TPU v7x, 512 devices: a whole 4x4x16 slice. The times are simulated.
512 devices in a mesh: lon: 32 (over y_hi, z), lat: 16 (over x, y_lo, core).
Axes of the slice: x: 4, y: 4 (y_hi: 2, y_lo: 2; y = y_hi * 2 + y_lo), z: 16, core: 2. Of those that a mesh axis runs over, the one named last changes fastest.
Arguments:
- inputs: bfloat16 [2, 96, 384, 192], P(None, 'lat', 'lon'), may hold values from -6 to 6
- cotangent: bfloat16 [2, 96, 384, 192], P(None, 'lat', 'lon'), may hold values from -6 to 6
- w_qkv: bfloat16 [2, 192, 576], replicated, may hold values from -0.4375 to 0.4375
- w_proj: bfloat16 [2, 192, 192], replicated, may hold values from -0.4375 to 0.4375
- w_up: bfloat16 [2, 192, 768], replicated, may hold values from -0.4375 to 0.4375
- w_down: bfloat16 [2, 768, 192], replicated, may hold values from -0.21875 to 0.21875
- earth_bias: float32 [2, 16, 1, 6, 3312], P(None, 'lat'), may hold values from -4 to 392
Outputs:
- result: bfloat16 [2, 96, 384, 192], P(None, 'lat', 'lon')
- grad_inputs: bfloat16 [2, 96, 384, 192], P(None, 'lat', 'lon')
- grad_qkv: float32 [2, 192, 576], P(None, 'lon')
- grad_proj: float32 [2, 192, 192], P(None, 'lon')
- grad_up: float32 [2, 192, 768], P(None, 'lon')
- grad_down: float32 [2, 768, 192], P(None, 'lon')
- grad_bias: float32 [2, 16, 1, 6, 3312], P(None, 'lat')
All inputs are finite; a program needn't handle non-finite values.
Results may differ from a plain program's by a relative error of at most 0.04.
Values may be sent and summed in bfloat16 or wider, within the bound.
A program may use at most 64 MiB of HBM per device.

v0:
```python
import jax
import jax.numpy as jnp
from jax import lax
from jax.sharding import PartitionSpec as P

HEADS = 6
WZ = 2
WLAT = 6
WLON = 12


NEG_FILL = -1e30
LN_EPS = 1e-05
INV_SQRT2 = 0.7071067811865476
INV_SQRT_2PI = 0.3989422804014327


def passed_along(value, axis, steps):
    count = lax.axis_size(axis)
    pairs = [(source, (source + steps) % count) for source in range(count)]
    return lax.ppermute(value, axis, pairs)


def product(spec_text, left_side, right_side):
    return jnp.einsum(spec_text, left_side, right_side, preferred_element_type=jnp.float32)


def outer_sum(left_side, right_side):
    left_flat = left_side.reshape(-1, left_side.shape[-1])
    right_flat = right_side.reshape(-1, right_side.shape[-1])
    return lax.dot_general(
        left_flat, right_flat, (((0,), (0,)), ((), ())), preferred_element_type=jnp.float32
    )


def to_windows(grid_field):
    levels, lat_rows, lon_cols, feat_width = grid_field.shape
    shaped = grid_field.reshape(
        levels // WZ, WZ, lat_rows // WLAT, WLAT, lon_cols // WLON, WLON, feat_width
    )
    shaped = shaped.transpose(0, 2, 4, 1, 3, 5, 6)
    return shaped.reshape(
        levels // WZ, lat_rows // WLAT, lon_cols // WLON, WZ * WLAT * WLON, feat_width
    )


def from_windows(windows):
    lev_win, lat_win, lon_win, tokens_win, feat_width = windows.shape
    shaped = windows.reshape(lev_win, lat_win, lon_win, WZ, WLAT, WLON, feat_width)
    shaped = shaped.transpose(0, 3, 1, 4, 2, 5, 6)
    return shaped.reshape(lev_win * WZ, lat_win * WLAT, lon_win * WLON, feat_width)


def offset_table():
    query_lon = jnp.arange(WLON)[:, None, None]
    key_lon = jnp.arange(WLON)[None, :, None]
    offsets = jnp.arange(2 * WLON - 1)[None, None, :]
    return (key_lon - query_lon + WLON - 1 == offsets).astype(jnp.float32)


def expand_bias(bias_table, onehot):
    lead_shape = bias_table.shape[:-1]
    zone_len = WZ * WLAT
    shaped = bias_table.reshape(lead_shape + (zone_len, zone_len, 2 * WLON - 1))
    full_bias = jnp.einsum("...abr,ijr->...aibj", shaped, onehot, precision=lax.Precision.HIGHEST)
    return full_bias.reshape(lead_shape + (zone_len * WLON, zone_len * WLON))


def fold_bias(grad_full, onehot):
    lead_shape = grad_full.shape[:-2]
    zone_len = WZ * WLAT
    shaped = grad_full.reshape(lead_shape + (zone_len, WLON, zone_len, WLON))
    folded = jnp.einsum("...aibj,ijr->...abr", shaped, onehot, precision=lax.Precision.HIGHEST)
    return folded.reshape(lead_shape + (zone_len * zone_len * (2 * WLON - 1),))


def region_labels(levels_win, last_lat):
    token_pos = jnp.arange(WZ * WLAT * WLON)
    level_in = token_pos // (WLAT * WLON)
    lat_in = token_pos // WLON % WLAT
    lev_last = (jnp.arange(levels_win) == levels_win - 1)[:, None, None]
    level_part = lev_last & (level_in == WZ - 1)[None, None, :]
    lat_part = last_lat[None, :, None] & (lat_in >= WLAT // 2)[None, None, :]
    return level_part.astype(jnp.int32) * 2 + lat_part.astype(jnp.int32)


def normalize(values_in):
    mean_val = jnp.mean(values_in, axis=-1, keepdims=True)
    centred = values_in - mean_val
    variance = jnp.mean(centred * centred, axis=-1, keepdims=True)
    inv_std = lax.rsqrt(variance + LN_EPS)
    return (centred * inv_std, inv_std)


def normalize_back(scaled, inv_std, grad_out):
    mean_grad = jnp.mean(grad_out, axis=-1, keepdims=True)
    mean_proj = jnp.mean(grad_out * scaled, axis=-1, keepdims=True)
    return inv_std * (grad_out - mean_grad - scaled * mean_proj)


def gelu_exact(pre_vals):
    return 0.5 * pre_vals * (1.0 + lax.erf(pre_vals * INV_SQRT2))


def gelu_slope(pre_vals):
    return (
        0.5 * (1.0 + lax.erf(pre_vals * INV_SQRT2))
        + pre_vals * jnp.exp(-0.5 * pre_vals * pre_vals) * INV_SQRT_2PI
    )


def move_lon(grid_field, step_dir):
    half_win = WLON // 2
    if step_dir > 0:
        strip_out = grid_field[:, :, :half_win]
    else:
        strip_out = grid_field[:, :, -half_win:]
    arrived = passed_along(strip_out, "lon", -step_dir)
    if step_dir > 0:
        return jnp.concatenate([grid_field[:, :, half_win:], arrived], axis=2)
    return jnp.concatenate([arrived, grid_field[:, :, :-half_win]], axis=2)


def move_lat(grid_field, step_dir):
    half_win = WLAT // 2
    if step_dir > 0:
        strip_out = grid_field[:, :half_win]
    else:
        strip_out = grid_field[:, -half_win:]
    arrived = passed_along(strip_out, "lat", -step_dir)
    if step_dir > 0:
        return jnp.concatenate([grid_field[:, half_win:], arrived], axis=1)
    return jnp.concatenate([arrived, grid_field[:, :-half_win]], axis=1)


def roll_field(grid_field, step_dir):
    grid_field = jnp.roll(grid_field, -step_dir, axis=0)
    return move_lat(move_lon(grid_field, step_dir), step_dir)


def block_forward(windows, weights, win_bias, labels):
    w_qkv, w_proj, w_up, w_down = weights
    lead_shape = windows.shape[:-1]
    feat_width = windows.shape[-1]
    head_dim = feat_width // HEADS
    score_scale = head_dim ** (-0.5)
    inputs_f = windows.astype(jnp.float32)
    scaled_one, inv_one = normalize(inputs_f)
    normed_one = scaled_one.astype(jnp.bfloat16)
    packed = product("...c,cd->...d", normed_one, w_qkv).astype(jnp.bfloat16)
    packed_t = jnp.moveaxis(packed.reshape(lead_shape + (3, HEADS, head_dim)), 3, -1)
    query_t = packed_t[:, :, :, 0]
    key_t = packed_t[:, :, :, 1]
    value_t = packed_t[:, :, :, 2]
    scores = product("laohdp,laohdq->laohpq", query_t, key_t) * score_scale + win_bias[:, :, None]
    if labels is not None:
        same_region = labels[:, :, None, None, :, None] == labels[:, :, None, None, None, :]
        scores = jnp.where(same_region, scores, NEG_FILL)
    row_top = jnp.max(scores, axis=-1, keepdims=True)
    exp_scores = jnp.exp(scores - row_top)
    attn_probs = exp_scores / jnp.sum(exp_scores, axis=-1, keepdims=True)
    attn_probs_b = attn_probs.astype(jnp.bfloat16)
    mixed_t = product("laohpq,laohdq->laohdp", attn_probs_b, value_t).astype(jnp.bfloat16)
    attn_mixed = jnp.moveaxis(mixed_t, -1, 3).reshape(lead_shape + (feat_width,))
    hidden_f = inputs_f + product("...c,cd->...d", attn_mixed, w_proj)
    hidden_b = lax.optimization_barrier(hidden_f.astype(jnp.bfloat16))
    scaled_two, inv_two = normalize(hidden_b.astype(jnp.float32))
    normed_two = scaled_two.astype(jnp.bfloat16)
    pre_act = product("...c,ck->...k", normed_two, w_up)
    active = gelu_exact(pre_act).astype(jnp.bfloat16)
    output = (hidden_b.astype(jnp.float32) + product("...k,kc->...c", active, w_down)).astype(
        jnp.bfloat16
    )
    saved_acts = (
        normed_one,
        scaled_one,
        inv_one,
        query_t,
        key_t,
        value_t,
        attn_probs,
        attn_probs_b,
        attn_mixed,
        scaled_two,
        inv_two,
        normed_two,
        pre_act,
        active,
    )
    return (output, saved_acts)


def block_backward(grad_out, saved_acts, weights):
    (
        normed_one,
        scaled_one,
        inv_one,
        query_t,
        key_t,
        value_t,
        attn_probs,
        attn_probs_b,
        attn_mixed,
        scaled_two,
        inv_two,
        normed_two,
        pre_act,
        active,
    ) = saved_acts
    w_qkv, w_proj, w_up, w_down = weights
    lead_shape = grad_out.shape[:-1]
    feat_width = grad_out.shape[-1]
    head_dim = feat_width // HEADS
    score_scale = head_dim ** (-0.5)
    grad_down = outer_sum(active, grad_out)
    grad_act = product("...c,kc->...k", grad_out, w_down)
    grad_pre = (grad_act * gelu_slope(pre_act)).astype(jnp.bfloat16)
    grad_up = outer_sum(normed_two, grad_pre)
    grad_norm_two = product("...k,ck->...c", grad_pre, w_up)
    grad_hidden = grad_out.astype(jnp.float32) + normalize_back(scaled_two, inv_two, grad_norm_two)
    grad_hidden_b = grad_hidden.astype(jnp.bfloat16)
    grad_proj = outer_sum(attn_mixed, grad_hidden_b)
    grad_mixed = product("...d,cd->...c", grad_hidden_b, w_proj).astype(jnp.bfloat16)
    grad_mixed_t = jnp.moveaxis(grad_mixed.reshape(lead_shape + (HEADS, head_dim)), 3, -1)
    grad_probs = product("laohdp,laohdq->laohpq", grad_mixed_t, value_t)
    grad_values = product("laohpq,laohdp->laohdq", attn_probs_b, grad_mixed_t)
    grad_scores = attn_probs * (
        grad_probs - jnp.sum(grad_probs * attn_probs, axis=-1, keepdims=True)
    )
    grad_bias = jnp.sum(grad_scores, axis=2)
    grad_scores_b = grad_scores.astype(jnp.bfloat16)
    grad_query = product("laohpq,laohdq->laohdp", grad_scores_b, key_t) * score_scale
    grad_keys = product("laohpq,laohdp->laohdq", grad_scores_b, query_t) * score_scale
    grad_packed_t = jnp.stack([grad_query, grad_keys, grad_values], axis=3)
    grad_packed = (
        jnp.moveaxis(grad_packed_t, -1, 3)
        .reshape(lead_shape + (3 * feat_width,))
        .astype(jnp.bfloat16)
    )
    grad_qkv = outer_sum(normed_one, grad_packed)
    grad_norm_one = product("...d,cd->...c", grad_packed, w_qkv)
    grad_in = (grad_hidden + normalize_back(scaled_one, inv_one, grad_norm_one)).astype(
        jnp.bfloat16
    )
    return (grad_in, (grad_qkv, grad_proj, grad_up, grad_down), grad_bias)


def on_device(inputs, cotangent, w_qkv, w_proj, w_up, w_down, earth_bias):
    onehot = offset_table()
    levels_win = inputs.shape[0] // WZ
    lat_win = inputs.shape[1] // WLAT
    lat_count = lax.axis_size("lat")
    lon_count = lax.axis_size("lon")
    total_tokens = inputs.shape[0] * inputs.shape[1] * inputs.shape[2] * lat_count * lon_count
    norm_scale = total_tokens ** (-0.5)
    last_lat = (jnp.arange(lat_win) == lat_win - 1) & (lax.axis_index("lat") == lat_count - 1)
    shift_labels = region_labels(levels_win, last_lat)
    weights_one = (w_qkv[0], w_proj[0], w_up[0], w_down[0])
    weights_two = (w_qkv[1], w_proj[1], w_up[1], w_down[1])
    bias_one = expand_bias(earth_bias[0], onehot).transpose(1, 0, 2, 3, 4)
    bias_two = expand_bias(earth_bias[1], onehot).transpose(1, 0, 2, 3, 4)
    first_out, saved_one = block_forward(to_windows(inputs), weights_one, bias_one, None)
    second_in = to_windows(roll_field(from_windows(first_out), 1))
    second_out, saved_two = block_forward(second_in, weights_two, bias_two, shift_labels)
    result = roll_field(from_windows(second_out), -1)
    grad_rolled = to_windows(roll_field(cotangent, 1))
    grad_second, grads_two, bias_grad_two = block_backward(grad_rolled, saved_two, weights_two)
    grad_mid = to_windows(roll_field(from_windows(grad_second), -1))
    grad_first, grads_one, bias_grad_one = block_backward(grad_mid, saved_one, weights_one)
    grad_inputs = from_windows(grad_first)
    stacked = tuple(
        (
            jnp.stack([one_grad * norm_scale, two_grad * norm_scale])
            for one_grad, two_grad in zip(grads_one, grads_two)
        )
    )
    summed = (
        lax.psum(stacked[0].astype(jnp.bfloat16), "lat").astype(jnp.float32),
        lax.psum(stacked[1].astype(jnp.bfloat16), "lat").astype(jnp.float32),
        lax.psum(stacked[2].astype(jnp.bfloat16), "lat").astype(jnp.float32),
        lax.psum(stacked[3].astype(jnp.bfloat16), "lat").astype(jnp.float32),
    )
    totals = (
        lax.psum_scatter(
            summed[0].astype(jnp.bfloat16), "lon", scatter_dimension=1, tiled=True
        ).astype(jnp.float32),
        lax.psum_scatter(
            summed[1].astype(jnp.bfloat16), "lon", scatter_dimension=1, tiled=True
        ).astype(jnp.float32),
        lax.psum_scatter(
            summed[2].astype(jnp.bfloat16), "lon", scatter_dimension=1, tiled=True
        ).astype(jnp.float32),
        lax.psum_scatter(
            summed[3].astype(jnp.bfloat16), "lon", scatter_dimension=1, tiled=True
        ).astype(jnp.float32),
    )
    bias_local = jnp.stack(
        [
            fold_bias(bias_grad_one, onehot).transpose(1, 0, 2, 3),
            fold_bias(bias_grad_two, onehot).transpose(1, 0, 2, 3),
        ]
    )
    grad_bias = lax.psum(bias_local.astype(jnp.bfloat16), "lon").astype(jnp.float32)
    return (result, grad_inputs, totals[0], totals[1], totals[2], totals[3], grad_bias)


def solution(mesh):
    return jax.shard_map(
        on_device,
        mesh=mesh,
        in_specs=(
            P(None, "lat", "lon", None),
            P(None, "lat", "lon", None),
            P(),
            P(),
            P(),
            P(),
            P(None, "lat", None, None, None),
        ),
        out_specs=(
            P(None, "lat", "lon", None),
            P(None, "lat", "lon", None),
            P(None, "lon", None),
            P(None, "lon", None),
            P(None, "lon", None),
            P(None, "lon", None),
            P(None, "lat", None, None, None),
        ),
        check_vma=False,
    )
```

profile of v0, /device:TPU:1, one launch (start us, length us, event | category | flops | bytes accessed | tf_op | source)
XLA Modules:
  0.0 549.7 jit_solution(11455561619086028189)
XLA Ops:
  13.1 4.9 convolution_bitcast_fusion.1
  17.9 11.7 %copy.232 = f32[1,1,6,12,12,12,12]{4,3,6,5,2,1,0:T(8,128)} copy(f32[1,1,6,12,12,12,12]{5,6,3,2,4,1,0:T(8,128)} %convolution_bitcast_fusion.1) | data formatting | bytes 995328 | tf_op jit(solution)/shard_map/broadcast_in_dim;transpose;reshape | solution.py:155
  29.7 5.0 reshape.999
  36.7 2.0 multiply_convert_fusion.1
  40.1 14.6 %collective-permute-start = (bf16[2,6,6,192]{3,2,1,0:T(8,128)(2,1)S(1)}, bf16[2,6,6,192]{3,2,1,0:T(8,128)(2,1)S(1)}, u32[]{:S(2)}, u32[]{:S(2)}) collective-permute-start(bf16[2,6,6,192]{3,2,1,0:T(8,128)(2,1)S(1)} %get-tuple-element.71), channel_id=1, source_target_pairs={{0,496},{16,0},{32,16},{48,32},{64,48},{80,64},{96,80},{112,96},{1... | collective-permute-start | bytes 82952 | tf_op jit(solution)/shard_map/ppermute | solution.py:21
  55.7 2.6 collective-permute-start.4
  59.4 4.9 convolution_bitcast_fusion
  64.3 11.7 %copy.235 = f32[1,1,6,12,12,12,12]{4,3,6,5,2,1,0:T(8,128)} copy(f32[1,1,6,12,12,12,12]{5,6,3,2,4,1,0:T(8,128)} %convolution_bitcast_fusion) | data formatting | bytes 995328 | tf_op jit(solution)/shard_map/broadcast_in_dim;transpose;reshape | solution.py:155
  76.0 5.0 reshape.1001
  81.0 3.1 collective-permute-start.1
  85.7 3.8 collective-permute-start.5
  97.5 1.9 convolution_convert_fusion.4
  101.2 2.1 multiply_convert_fusion
  112.4 2.4 fusion.103
  118.8 1.7 convolution_convert_fusion.7
  122.2 1.9 fusion.41
  128.5 5.0 reshape.982
  135.9 1.7 fusion.23
  137.7 2.0 fusion.21
  140.7 2.8 collective-permute-start.6
  143.5 6.0 %fusion.10 = bf16[6,12,12,23]{3,1,2,0:T(8,128)(2,1)S(1)} fusion(f32[6,12,12,12,12]{2,1,4,3,0:T(8,128)} %reshape.982, s32[12,12]{0,1:T(8,128)S(1)} %subtract_add_fusion), kind=kOutput, calls=%fused_computation.22 | convolution fusion | flops 34362000 | bytes 537984 | tf_op jit(solution)/shard_map/...aibj,ijr->...abr/dot_general | solution.py:73
  149.4 1.9 fusion.19
  151.4 2.4 collective-permute-start.7
  163.7 5.0 reshape.981
  170.3 1.8 copy.211
  172.1 6.0 %fusion.9 = bf16[6,12,12,23]{3,1,2,0:T(8,128)(2,1)S(1)} fusion(f32[6,12,12,12,12]{2,1,4,3,0:T(8,128)} %reshape.981, s32[12,12]{0,1:T(8,128)S(1)} %subtract_add_fusion), kind=kOutput, calls=%fused_computation.21 | convolution fusion | flops 34362000 | bytes 537984 | tf_op jit(solution)/shard_map/...aibj,ijr->...abr/dot_general | solution.py:73
  185.8 1.9 collective-permute-start.2
  190.3 3.8 collective-permute-done.2
  194.3 4.6 collective-permute-start.3
  200.3 2.7 collective-permute-done.3
  203.7 261.2 %all-reduce.8.cloned.1.call-done = (bf16[2,768,192]{2,0,1:T(2,128)(2,1)}, bf16[2,1,1,6,3312]{4,3,2,1,0:T(8,128)(2,1)}, bf16[2,192,576]{2,0,1:T(2,128)(2,1)}, bf1...) async-done(((bf16[2,768,192]{2,0,1:T(2,128)(2,1)}, bf16[2,1,1,6,3312]{4,3,2,1,0:T(8,128)(2,1)}, bf16[2,192,576]{2,0,1:T(2,128)(2,1)}, bf16[2,192,192]{2,0,1:T(2,128)(2,1)}, ...) | async-done | bytes 1848976
  467.9 70.8 %all-reduce.5 = (bf16[2,24,192]{2,0,1:T(2,128)(2,1)S(1)}, bf16[2,6,576]{2,0,1:T(2,128)(2,1)S(1)}, bf16[2,6,192]{2,0,1:T(2,128)(2,1)S(1)}, bf16[2,6,768]{2,0,1:T(2,128)(2,1)S(1)}) all-reduce(bf16[2,24,192]{2,0,1:T(2,128)(2,1)S(1)} %constant_dynamic-slice_fusion, ...), channel_id=1, replica_groups=mesh['lon'=32,'lat'=16] {'lat'}, use_global_device_ids=true, to_apply=%region_28.29 | all-reduce | flops 27648 | bytes 110592 | tf_op jit(solution)/shard_map/psum | solution.py:281
  (242 shorter events, 74.2 us)
Async XLA Ops:
  7.2 457.8 %all-reduce.8.cloned.1.call-start = ((), (), s32[]{:S(2)}) async-start(), calls=%async_computation | async-start | bytes 4341760
  8.1 28.0 %copy-start = (f32[144,192]{1,0:T(8,128)}, f32[144,192]{1,0:T(8,128)S(1)}, u32[]{:S(2)}) copy-start(f32[144,192]{1,0:T(8,128)S(1)} %reshape.983) | copy-start | bytes 331780
  11.2 24.6 %copy-start.11 = (bf16[144,576]{0,1:T(8,128)(2,1)}, bf16[144,576]{0,1:T(8,128)(2,1)S(1)}, u32[]{:S(2)}) copy-start(bf16[144,576]{0,1:T(8,128)(2,1)S(1)} %copy.184) | copy-start | bytes 497668
  34.6 20.1 %copy-start.30 = (bf16[2,6,12,192]{3,0,2,1:T(2,128)(2,1)S(1)}, bf16[2,6,12,192]{3,0,2,1:T(2,128)(2,1)}, u32[]{:S(2)}) copy-start(bf16[2,6,12,192]{3,0,2,1:T(2,128)(2,1)} %param.8) | copy-start | bytes 165892
  35.8 28.5 %copy-start.34 = (f32[6,144]{1,0:T(8,128)}, f32[6,144]{1,0:T(8,128)S(1)}, u32[]{:S(2)}) copy-start(f32[6,144]{1,0:T(8,128)S(1)} %get-tuple-element.86) | copy-start | bytes 10372
  36.1 22.2 %copy-start.25 = (bf16[6,32,144]{2,1,0:T(8,128)(2,1)}, bf16[6,32,144]{2,1,0:T(8,128)(2,1)S(1)}, u32[]{:S(2)}) copy-start(bf16[6,32,144]{2,1,0:T(8,128)(2,1)S(1)} %convolution_convert_fusion.5) | copy-start | bytes 165892
  36.5 27.8 %copy-start.39 = (f32[144]{0:T(256)}, f32[144]{0:T(256)S(1)}, u32[]{:S(2)}) copy-start(f32[144]{0:T(256)S(1)} %broadcast_multiply_fusion.11) | copy-start | bytes 1732
  36.7 27.6 %copy-start.42 = (f32[144]{0:T(256)}, f32[144]{0:T(256)S(1)}, u32[]{:S(2)}) copy-start(f32[144]{0:T(256)S(1)} %add_rsqrt_fusion.2) | copy-start | bytes 1732
  40.1 40.8 %collective-permute-start = (bf16[2,6,6,192]{3,2,1,0:T(8,128)(2,1)S(1)}, bf16[2,6,6,192]{3,2,1,0:T(8,128)(2,1)S(1)}, u32[]{:S(2)}, u32[]{:S(2)}) collective-permute-start(bf16[2,6,6,192]{3,2,1,0:T(8,128)(2,1)S(1)} %get-tuple-element.71), channel_id=1, source_target_pairs={{0,496},{16,0},{32,16},{48,32},{64,48},{80,64},{96,80},{112,96},{1... | collective-permute-start | bytes 82952 | tf_op jit(solution)/shard_map/ppermute | solution.py:21
  55.7 28.5 %collective-permute-start.4 = (bf16[2,6,6,192]{3,0,2,1:T(2,128)(2,1)}, bf16[2,6,6,192]{3,0,2,1:T(2,128)(2,1)}, u32[]{:S(2)}, u32[]{:S(2)}) collective-permute-start(bf16[2,6,6,192]{3,0,2,1:T(2,128)(2,1)} %get-tuple-element.65), channel_id=1, source_target_pairs={{0,496},{16,0},{32,16},{48,32},{64,48},{80,64},{96,80},{112,96},{1... | collective-permute-start | bytes 82952 | tf_op jit(solution)/shard_map/ppermute | solution.py:21
  76.0 17.7 %copy-start.5 = (bf16[2,192,576]{2,1,0:T(8,128)(2,1)S(1)}, bf16[2,192,576]{2,1,0:T(8,128)(2,1)}, u32[]{:S(2)}) copy-start(bf16[2,192,576]{2,1,0:T(8,128)(2,1)} %param.9) | copy-start | bytes 1327108
  81.0 8.5 %collective-permute-start.1 = (bf16[2,3,12,192]{3,2,1,0:T(8,128)(2,1)S(1)}, bf16[2,3,12,192]{3,2,1,0:T(8,128)(2,1)S(1)}, u32[]{:S(2)}, u32[]{:S(2)}) collective-permute-start(bf16[2,3,12,192]{3,2,1,0:T(8,128)(2,1)S(1)} %get-tuple-element.69), channel_id=1, source_target_pairs={{0,15},{1,0},{2,1},{3,2},{4,3},{5,4},{6,5},{7,6},{8,7},{9,8},{10,9... | collective-permute-start | bytes 82952 | tf_op jit(solution)/shard_map/ppermute | solution.py:21
  85.7 17.6 %collective-permute-start.5 = (bf16[2,3,12,192]{3,0,2,1:T(2,128)(2,1)}, bf16[2,3,12,192]{3,0,2,1:T(2,128)(2,1)}, u32[]{:S(2)}, u32[]{:S(2)}) collective-permute-start(bf16[2,3,12,192]{3,0,2,1:T(2,128)(2,1)} %get-tuple-element.77), channel_id=1, source_target_pairs={{0,15},{1,0},{2,1},{3,2},{4,3},{5,4},{6,5},{7,6},{8,7},{9,8},{10,9... | collective-permute-start | bytes 82952 | tf_op jit(solution)/shard_map/ppermute | solution.py:21
  126.1 13.6 %copy-start.2 = (f32[144,192]{1,0:T(8,128)S(1)}, f32[144,192]{1,0:T(8,128)}, u32[]{:S(2)}) copy-start(f32[144,192]{1,0:T(8,128)} %reshape.986) | copy-start | bytes 331780
  126.1 13.6 %copy-start.4 = (f32[1,1,1,144,192]{4,3,2,1,0:T(8,128)S(1)}, f32[1,1,1,144,192]{4,3,2,1,0:T(8,128)}, u32[]{:S(2)}) copy-start(f32[1,1,1,144,192]{4,3,2,1,0:T(8,128)} %copy-done.3) | copy-start | bytes 331780
  133.4 16.0 %copy-start.20 = (bf16[144,768]{1,0:T(8,128)(2,1)S(1)}, bf16[144,768]{1,0:T(8,128)(2,1)}, u32[]{:S(2)}) copy-start(bf16[144,768]{1,0:T(8,128)(2,1)} %get-tuple-element.92) | copy-start | bytes 663556
  133.4 20.4 %copy-start.27 = (bf16[6,32,144]{2,1,0:T(8,128)(2,1)S(1)}, bf16[6,32,144]{2,1,0:T(8,128)(2,1)}, u32[]{:S(2)}) copy-start(bf16[6,32,144]{2,1,0:T(8,128)(2,1)} %convolution_convert_fusion.4) | copy-start | bytes 165892
  135.9 21.8 %copy-start.8 = (bf16[1,1,1,144,192]{4,3,2,1,0:T(8,128)(2,1)S(1)}, bf16[1,1,1,144,192]{4,3,2,1,0:T(8,128)(2,1)}, u32[]{:S(2)}) copy-start(bf16[1,1,1,144,192]{4,3,2,1,0:T(8,128)(2,1)} %copy-done.7) | copy-start | bytes 165892
  135.9 21.8 %copy-start.40 = (f32[144]{0:T(256)S(1)}, f32[144]{0:T(256)}, u32[]{:S(2)}) copy-start(f32[144]{0:T(256)} %copy-done.39) | copy-start | bytes 1732
  135.9 21.8 %copy-start.43 = (f32[144]{0:T(256)S(1)}, f32[144]{0:T(256)}, u32[]{:S(2)}) copy-start(f32[144]{0:T(256)} %copy-done.42) | copy-start | bytes 1732
  139.7 19.7 %copy-start.23 = (bf16[2,192,192]{2,1,0:T(8,128)(2,1)S(1)}, bf16[2,192,192]{2,1,0:T(8,128)(2,1)}, u32[]{:S(2)}) copy-start(bf16[2,192,192]{2,1,0:T(8,128)(2,1)} %param.10) | copy-start | bytes 442372
  140.5 15.9 %copy-start.24 = (f32[144,768]{1,0:T(8,128)S(1)}, f32[144,768]{1,0:T(8,128)}, u32[]{:S(2)}) copy-start(f32[144,768]{1,0:T(8,128)} %get-tuple-element.89) | copy-start | bytes 1327108
  140.6 19.2 %copy-start.35 = (f32[6,144]{1,0:T(8,128)S(1)}, f32[6,144]{1,0:T(8,128)}, u32[]{:S(2)}) copy-start(f32[6,144]{1,0:T(8,128)} %copy-done.34) | copy-start | bytes 10372
  140.7 20.0 %copy-start.12 = (bf16[144,576]{0,1:T(8,128)(2,1)S(1)}, bf16[144,576]{0,1:T(8,128)(2,1)}, u32[]{:S(2)}) copy-start(bf16[144,576]{0,1:T(8,128)(2,1)} %copy-done.11) | copy-start | bytes 497668
  140.7 10.7 %collective-permute-start.6 = (bf16[2,6,6,192]{3,2,1,0:T(8,128)(2,1)S(1)}, bf16[2,6,6,192]{3,2,1,0:T(8,128)(2,1)S(1)}, u32[]{:S(2)}, u32[]{:S(2)}) collective-permute-start(bf16[2,6,6,192]{3,2,1,0:T(8,128)(2,1)S(1)} %get-tuple-element.66), channel_id=1, source_target_pairs={{0,16},{16,32},{32,48},{48,64},{64,80},{80,96},{96,112},{112,128},... | collective-permute-start | bytes 82952 | tf_op jit(solution)/shard_map/ppermute | solution.py:21
  151.4 4.2 collective-permute-start.7
  170.3 11.9 %copy-start.31 = (bf16[1,192,768]{2,1,0:T(8,128)(2,1)S(1)}, bf16[1,192,768]{2,1,0:T(8,128)(2,1)}, u32[]{:S(2)}) copy-start(bf16[1,192,768]{2,1,0:T(8,128)(2,1)} %fusion.21) | copy-start | bytes 884740
  172.1 12.3 %copy-start.21 = (bf16[144,768]{1,0:T(8,128)(2,1)S(1)}, bf16[144,768]{1,0:T(8,128)(2,1)}, u32[]{:S(2)}) copy-start(bf16[144,768]{1,0:T(8,128)(2,1)} %get-tuple-element.92) | copy-start | bytes 663556
  178.1 20.9 %copy-start.1 = (f32[144,192]{1,0:T(8,128)S(1)}, f32[144,192]{1,0:T(8,128)}, u32[]{:S(2)}) copy-start(f32[144,192]{1,0:T(8,128)} %copy-done) | copy-start | bytes 331780
  178.1 20.9 %copy-start.6 = (bf16[2,192,576]{2,1,0:T(8,128)(2,1)S(1)}, bf16[2,192,576]{2,1,0:T(8,128)(2,1)}, u32[]{:S(2)}) copy-start(bf16[2,192,576]{2,1,0:T(8,128)(2,1)} %param.9) | copy-start | bytes 1327108
  185.8 8.3 %collective-permute-start.2 = (bf16[2,6,6,192]{3,0,2,1:T(2,128)(2,1)S(1)}, bf16[2,6,6,192]{3,0,2,1:T(2,128)(2,1)S(1)}, u32[]{:S(2)}, u32[]{:S(2)}) collective-permute-start(bf16[2,6,6,192]{3,0,2,1:T(2,128)(2,1)S(1)} %fusion.142), channel_id=1, source_target_pairs={{0,16},{16,32},{32,48},{48,64},{64,80},{80,96},{96,112},{112,128},... | collective-permute-start | bytes 82952 | tf_op jit(solution)/shard_map/ppermute | solution.py:21
  194.3 8.7 %collective-permute-start.3 = (bf16[2,3,12,192]{3,0,2,1:T(2,128)(2,1)S(1)}, bf16[2,3,12,192]{3,0,2,1:T(2,128)(2,1)S(1)}, u32[]{:S(2)}, u32[]{:S(2)}) collective-permute-start(bf16[2,3,12,192]{3,0,2,1:T(2,128)(2,1)S(1)} %get-tuple-element.80), channel_id=1, source_target_pairs={{0,1},{1,2},{2,3},{3,4},{4,5},{5,6},{6,7},{7,8},{8,9},{9,10},{10,1... | collective-permute-start | bytes 82952 | tf_op jit(solution)/shard_map/ppermute | solution.py:21
  (24 other events, 120.4 us)
Sparse Core Ops, SparseCore 0:
  184.5 280.3 all-reduce.7
where the time goes:
time: 553 us; the launch traced here: 550 us
  waiting for transfers between devices  268 us (48%)
  local copies, waits for them, and re-layouts  72.5 us (13%)
  blocking collectives  70.8 us (13%)
  matrix products  62.1 us (11%)
  starting transfers between devices  35.9 us (6%)
  other arithmetic  23.5 us (4%)
  between operations  16.6 us (3%)
    unnamed x2, waiting for transfers between devices  261 us
    psum x1, blocking collectives, on_device(): lax.psum(stacked[3].astype(jnp.bfloat16), 'lat').astype(jnp.float32)  70.8 us
    ppermute x8, starting transfers between devices, passed_along(): return lax.ppermute(value, axis, pairs)  35.9 us
    another operation x4, local copies, waits for them, and re-layouts, block_forward(): win_bias[:, :, None]  33.4 us
    dot_general x28, matrix products, product(): jnp.einsum(spec_text, left_side, right_side, preferred_element_type=jnp.f...  30.7 us
    another operation x8, local copies, waits for them, and re-layouts  12.3 us
    dot_general x2, matrix products, fold_bias(): jnp.einsum('...aibj,ijr->...abr', shaped, onehot, precision=lax.Precision...  12 us
  transfers between devices with their start and end apart: 9, of which 4 were waited for; matrix products, arithmetic and copies ran while one was open for 9% of the time, Pallas kernels for 0%

commit v1 on v0

v1 whole, which is shorter than its diff:
```python
import jax
import jax.numpy as jnp
from jax import lax
from jax.experimental import pallas as pl
from jax.experimental.pallas import tpu as pltpu
from jax.sharding import PartitionSpec as P

BF = jnp.bfloat16
F32 = jnp.float32
MESH = pl.DeviceIdType.MESH

HEADS = 6
C = 192
HID = 768
WLON = 12
ZONES = 12
REACH = 23
TAB = ZONES * REACH
NLAT = 16
NLON = 32
SHARD = 6
TOK = 192
NEG_FILL = -1e30
LN_EPS = 1e-05
SCALE = 32.0 ** -0.5
NORM = 73728.0 ** -0.5

QPOS = [c if c < 6 else c + 2 for c in range(WLON)]
PAD_POS = [6, 7, 14, 15]


def nn(a, b):
    return lax.dot_general(a, b, (((1,), (0,)), ((), ())), preferred_element_type=F32)


def nt(a, b):
    return lax.dot_general(a, b, (((1,), (1,)), ((), ())), preferred_element_type=F32)


def iota(shape, dim):
    return lax.broadcasted_iota(jnp.int32, shape, dim)


def onehot(cond):
    return jnp.where(cond, 1.0, 0.0).astype(BF)


def ln(x):
    mean = jnp.mean(x, axis=-1, keepdims=True)
    centred = x - mean
    inv = lax.rsqrt(jnp.mean(centred * centred, axis=-1, keepdims=True) + LN_EPS)
    return centred * inv, inv


def ln_back(scaled, inv, grad):
    mean_grad = jnp.mean(grad, axis=-1, keepdims=True)
    mean_proj = jnp.mean(grad * scaled, axis=-1, keepdims=True)
    return inv * (grad - mean_grad - scaled * mean_proj)


def gelu_pair(v):
    gauss = jnp.exp(-0.5 * v * v)
    t = 1.0 / (1.0 + (0.3275911 * 0.7071067811865476) * jnp.abs(v))
    poly = t * (
        0.127414796 + t * (-0.142248368 + t * (0.7107068705 + t * (-0.7265760135 + t * 0.5307027145)))
    )
    tail = poly * gauss
    phi = jnp.where(v < 0.0, tail, 1.0 - tail)
    return v * phi, phi + v * gauss * 0.3989422804014327


def key_target(lanes, width, shape, dim):
    y = iota(shape, dim)
    pos = y & 15
    col = jnp.where(pos < 8, pos, pos - 2)
    valid = ((pos & 7) < 6) & (y < lanes)
    return jnp.where(valid, (y >> 4) * REACH + col + (WLON - 1), -1)


def kernel(
    x_ref, ct_ref, wqkv_ref, wproj_ref, wup_ref, wdown_ref, eb_ref,
    res_ref, gin_ref, oqkv_ref, oproj_ref, oup_ref, odown_ref, obias_ref,
    win_ref, n1_ref, sc1_ref, inv1_ref, qkv_ref, p1_ref, p2_ref, mix_ref, sc2_ref, inv2_ref, n2_ref,
    act_ref, slope_ref, gpre_ref, gqkv_ref, ghb_ref, g_ref,
    t_ref, bias1_ref, bias2_ref, ds1_ref, ds2_ref,
    perm_ref, sel_ref,
    xs_ref, xr_ref,
    strip_ref, r1_ref, s2_ref, r2_ref, s3_ref, r3_ref,
    bs_ref, br_ref, ball_ref,
    x_send, x_recv, s1_send, s1_recv, s2_send, s2_recv, s3_send, s3_recv, b_send, b_recv, bg_send, bg_recv,
):
    lat = lax.axis_index("lat")
    lon = lax.axis_index("lon")

    def at_lat(k):
        return lax.rem(lat + k + NLAT, NLAT)

    def at_lon(k):
        return lax.rem(lon + k + NLON, NLON)

    barrier = pltpu.get_barrier_semaphore()

    def greet_lat(k, carry):
        pl.semaphore_signal(barrier, inc=1, device_id={"lat": at_lat(k)}, device_id_type=MESH)
        return carry

    def greet_lon(k, carry):
        pl.semaphore_signal(barrier, inc=1, device_id={"lon": at_lon(k)}, device_id_type=MESH)
        return carry

    lax.fori_loop(1, NLAT, greet_lat, 0)
    lax.fori_loop(1, NLON, greet_lon, 0)
    for k in (-1, 1):
        pl.semaphore_signal(
            barrier, inc=1, device_id={"lat": at_lat(k), "lon": at_lon(k)}, device_id_type=MESH
        )

    lane = iota((1, C), 1) >> 5
    hm = [onehot(lane == h) for h in range(HEADS)]
    eye = onehot(iota((C, C), 0) == iota((C, C), 1))
    tgt1 = key_target(TOK, 256, (1, 256), 1)
    tgt2 = key_target(96, 128, (1, 128), 1)

    def load_window(src):
        for z in range(ZONES):
            v = src[z // 6, z % 6].astype(F32)
            win_ref[16 * z:16 * z + 16, :] = jnp.zeros((16, C), F32)
            win_ref[16 * z:16 * z + 6, :] = v[0:6]
            win_ref[16 * z + 8:16 * z + 14, :] = v[6:12]
        return win_ref[...]

    def store_window(dst, val):
        for z in range(ZONES):
            win_ref[16 * z:16 * z + 8, :] = val[16 * z:16 * z + 8]
            win_ref[16 * z + 6:16 * z + 14, :] = val[16 * z + 8:16 * z + 16]
            dst[z // 6, z % 6] = win_ref[16 * z:16 * z + 12, :].astype(BF)

    def group(val, lev, row, half):
        at = 96 * lev + 16 * row + 8 * half
        return val[at:at + 8]

    def strip(val, row0, half):
        return jnp.concatenate(
            [group(val, lev, row0 + r, half) for lev in range(2) for r in range(3)], axis=0
        ).astype(BF)

    def exchange_copies(idx):
        step = -1 if idx < 2 else 1
        targets = (
            {"lon": at_lon(step)},
            {"lat": at_lat(step)},
            {"lat": at_lat(step), "lon": at_lon(step)},
        )
        return [
            pltpu.make_async_remote_copy(
                src_ref=xs_ref.at[idx, i],
                dst_ref=xr_ref.at[idx, i],
                send_sem=x_send.at[idx, i],
                recv_sem=x_recv.at[idx, i],
                device_id=targets[i],
                device_id_type=MESH,
            )
            for i in range(3)
        ]

    def exchange_start(idx, val):
        if idx < 2:
            parts = (strip(val, 3, 0), strip(val, 0, 1), strip(val, 0, 0))
        else:
            parts = (strip(val, 0, 1), strip(val, 3, 0), strip(val, 3, 1))
        for i, copy in enumerate(exchange_copies(idx)):
            xs_ref[idx, i] = parts[i]
            copy.start()

    def exchange_finish(idx, val):
        for copy in exchange_copies(idx):
            copy.wait()
        got = [xr_ref[idx, i].astype(F32) for i in range(3)]
        row_near = 0 if idx < 2 else 3
        half_near = 0 if idx < 2 else 1
        rows = []
        for lev in range(2):
            old = 1 - lev
            for row in range(6):
                near_row = (row < 3) == (row_near == 0)
                r = row % 3
                pieces = []
                for half in range(2):
                    near_half = half == half_near
                    at = 24 * old + 8 * r
                    if near_row and near_half:
                        piece = group(val, old, (3 if idx < 2 else 0) + r, 1 - half)
                    elif near_row:
                        piece = got[0][at:at + 8]
                    elif near_half:
                        piece = got[1][at:at + 8]
                    else:
                        piece = got[2][at:at + 8]
                    pieces.append(piece)
                rows += pieces
        return jnp.concatenate(rows, axis=0)

    def load_table(b):
        t_ref[...] = jnp.zeros_like(t_ref)
        for a in range(ZONES):
            t_ref[8 * a:8 * a + 6, 0:TAB] = eb_ref[b, :, TAB * a:TAB * a + TAB]

    def split3(v):
        hi = v.astype(BF)
        rest = v - hi.astype(F32)
        mid = rest.astype(BF)
        return hi, mid, (rest - mid.astype(F32)).astype(BF)

    def expand_bias(b):
        load_table(b)
        table = t_ref[...]
        if b == 0:
            spread = [onehot(iota((384, 256), 0) == tgt1)]
            mask = jnp.broadcast_to(jnp.where(tgt1 < 0, NEG_FILL, 0.0), (96, 256))
        else:
            spread = [onehot(iota((384, 128), 0) == jnp.where(tgt2 < 0, -1, tgt2 + 138 * lv)) for lv in range(2)]
            zone = iota((96, 1), 0) >> 3
            zone = jnp.where(zone >= 6, zone - 6, zone)
            far_row = jnp.where(zone >= 3, 1, 0)
            far_key = jnp.where(iota((1, 128), 1) >= 48, 1, 0)
            last = jnp.where(lat == NLAT - 1, 1, 0)
            cut = (far_row + far_key) * last == 1
            mask = jnp.where(cut | (tgt2 < 0), NEG_FILL, 0.0)
        for c in range(WLON):
            rolled = pltpu.roll(table, c, 1) if c else table
            parts = split3(rolled)
            if b == 0:
                full = sum(nn(p, spread[0]) for p in parts) + mask
                for t in range(2):
                    bias1_ref[t, pl.ds(QPOS[c], 96, stride=16), :] = full[:, 128 * t:128 * t + 128]
            else:
                full = jnp.concatenate(
                    [sum(nn(p[48 * lv:48 * lv + 48], spread[lv]) for p in parts) for lv in range(2)], axis=0
                )
                bias2_ref[pl.ds(QPOS[c], 96, stride=16), :] = full + mask
        for p in PAD_POS:
            if b == 0:
                for t in range(2):
                    bias1_ref[t, pl.ds(p, 96, stride=16), :] = mask[:, 128 * t:128 * t + 128]
            else:
                bias2_ref[pl.ds(p, 96, stride=16), :] = mask

    def head_rows(ref, h, first, last):
        return jnp.concatenate(
            [ref[(8 * a + h) * 16:(8 * a + h) * 16 + 16, :] for a in range(first, last)], axis=0
        )

    def head_bias(b, h, seg):
        if b == 0:
            return jnp.concatenate(
                [head_rows(bias1_ref.at[0], h, 0, ZONES), head_rows(bias1_ref.at[1], h, 0, ZONES)[:, :64]], axis=1
            )
        return head_rows(bias2_ref, h, 6 * seg, 6 * seg + 6)[:, :96]

    segments = ((0, TOK),), ((0, 96), (96, 96))

    def forward(b, u):
        sc1, inv1 = ln(u)
        n1 = sc1.astype(BF)
        n1_ref[b] = n1
        sc1_ref[b] = sc1
        inv1_ref[b] = inv1
        qkv_ref[b] = nn(n1, wqkv_ref[b]).astype(BF)
        for seg, (start, size) in enumerate(segments[b]):
            q = qkv_ref[b, start:start + size, 0:C]
            k = qkv_ref[b, start:start + size, C:2 * C]
            v = qkv_ref[b, start:start + size, 2 * C:3 * C]
            mixed = jnp.zeros((size, C), F32)
            for h in range(HEADS):
                scores = nt(q * hm[h], k) * SCALE + head_bias(b, h, seg)
                top = jnp.max(scores, axis=-1, keepdims=True)
                e = jnp.exp(scores - top)
                probs = (e * (1.0 / jnp.sum(e, axis=-1, keepdims=True))).astype(BF)
                if b == 0:
                    p1_ref[h] = probs
                else:
                    p2_ref[h, start:start + size, :] = probs
                mixed = mixed + nn(probs, v * hm[h])
            mix_ref[b, start:start + size, :] = mixed.astype(BF)
        hidden = (u + nn(mix_ref[b], wproj_ref[b])).astype(BF).astype(F32)
        sc2, inv2 = ln(hidden)
        n2 = sc2.astype(BF)
        sc2_ref[b] = sc2
        inv2_ref[b] = inv2
        n2_ref[b] = n2
        acc = hidden
        for c in range(0, HID, 256):
            act, slope = gelu_pair(nn(n2, wup_ref[b, :, c:c + 256]))
            act = act.astype(BF)
            act_ref[b, :, c:c + 256] = act
            slope_ref[b, :, c:c + 256] = slope.astype(BF)
            acc = acc + nn(act, wdown_ref[b, c:c + 256, :])
        return acc.astype(BF).astype(F32)

    def backward_mlp(b, gf):
        g = gf.astype(BF)
        g_ref[b] = g
        gn2 = jnp.zeros((TOK, C), F32)
        for c in range(0, HID, 256):
            gact = nt(g, wdown_ref[b, c:c + 256, :])
            gpre = (gact * slope_ref[b, :, c:c + 256].astype(F32)).astype(BF)
            gpre_ref[b, :, c:c + 256] = gpre
            gn2 = gn2 + nt(gpre, wup_ref[b, :, c:c + 256])
        ghid = gf + ln_back(sc2_ref[b], inv2_ref[b], gn2)
        ghb_ref[b] = ghid.astype(BF)
        return ghid

    def backward_attention(b, ghid):
        gmix_all = nt(ghb_ref[b], wproj_ref[b]).astype(BF)
        for seg, (start, size) in enumerate(segments[b]):
            rows = slice(start, start + size)
            q = qkv_ref[b, rows, 0:C]
            k = qkv_ref[b, rows, C:2 * C]
            v = qkv_ref[b, rows, 2 * C:3 * C]
            gmix = gmix_all[rows]
            qt = nt(eye, q).astype(BF)
            gmt = nt(eye, gmix).astype(BF)
            gq = jnp.zeros((size, C), F32)
            gkt = []
            gvt = []
            for h in range(HEADS):
                pb = p1_ref[h] if b == 0 else p2_ref[h, rows, :]
                pf = pb.astype(F32)
                gp = nt(gmix * hm[h], v)
                ds = pf * (gp - jnp.sum(gp * pf, axis=-1, keepdims=True))
                if b == 0:
                    for a in range(ZONES):
                        at = (8 * a + h) * 16
                        ds1_ref[0, at:at + 16, :] = ds[16 * a:16 * a + 16, 0:128]
                        ds1_ref[1, at:at + 16, 0:64] = ds[16 * a:16 * a + 16, 128:192]
                else:
                    for a in range(6):
                        at = (8 * (a + 6 * seg) + h) * 16
                        ds2_ref[at:at + 16, 0:96] = ds[16 * a:16 * a + 16, :]
                dsb = ds.astype(BF)
                gq = gq + nn(dsb, k * hm[h])
                gkt.append(nn(qt[32 * h:32 * h + 32], dsb))
                gvt.append(nn(gmt[32 * h:32 * h + 32], pb))
            small = eye if size == C else eye[0:size, 0:size]
            gk = nt(small, (jnp.concatenate(gkt, axis=0) * SCALE).astype(BF)).astype(BF)
            gv = nt(small, jnp.concatenate(gvt, axis=0).astype(BF)).astype(BF)
            gqkv_ref[b, rows, 0:C] = (gq * SCALE).astype(BF)
            gqkv_ref[b, rows, C:2 * C] = gk
            gqkv_ref[b, rows, 2 * C:3 * C] = gv
        gn1 = nt(gqkv_ref[b], wqkv_ref[b])
        return (ghid + ln_back(sc1_ref[b], inv1_ref[b], gn1)).astype(BF).astype(F32)

    def put_strips(b, t, s, val):
        val = (val * NORM).astype(BF)
        for i in range(val.shape[1] // 128):
            strip_ref[b, t, s + i] = val[:, 128 * i:128 * i + 128]

    def grads_mlp(b):
        actt = nt(perm_ref[...], act_ref[b]).astype(BF)
        g = g_ref[b]
        for pair in range(2):
            at = 384 * pair
            both = [nn(actt[at + 192 * i:at + 192 * i + 192], g) for i in range(2)]
            put_strips(b, 0, 3 * pair, jnp.concatenate(both, axis=1))
        n2t = nt(eye, n2_ref[b]).astype(BF)
        for s in range(3):
            put_strips(b, 1, 2 * s, nn(n2t, gpre_ref[b, :, 256 * s:256 * s + 256]))

    def grads_attention(b):
        n1t = nt(eye, n1_ref[b]).astype(BF)
        mixt = nt(eye, mix_ref[b]).astype(BF)
        put_strips(b, 2, 0, nn(n1t, gqkv_ref[b, :, 0:256]))
        put_strips(b, 2, 2, nn(n1t, gqkv_ref[b, :, 256:512]))
        rest = [nn(n1t, gqkv_ref[b, :, 512:576]), nn(mixt, ghb_ref[b])]
        put_strips(b, 2, 4, jnp.concatenate(rest, axis=1))

    def place(b):
        return lat if b == 0 else NLAT - 1 - lat

    def owner(b, t, s):
        at = (2 * s, 2 * s + 1, (12 + 2 * s) % NLAT)[t]
        return at if b == 0 else NLAT - 1 - at

    def owned(b, t):
        at = place(b)
        if t == 0:
            return (lax.rem(at, 2) == 0) & (at < 12), at // 2
        if t == 1:
            return (lax.rem(at, 2) == 1) & (at < 12), at // 2
        back = lax.rem(at + 4, NLAT)
        return (lax.rem(back, 2) == 0) & (back < 12), back // 2

    def s1_copy(b, t, s):
        return pltpu.make_async_remote_copy(
            src_ref=strip_ref.at[b, t, s],
            dst_ref=r1_ref.at[b, t, lat],
            send_sem=s1_send.at[b, t, s],
            recv_sem=s1_recv.at[b, t],
            device_id={"lat": owner(b, t, s)},
            device_id_type=MESH,
        )

    def stage1_send(b, t):
        for s in range(6):
            @pl.when(lat != owner(b, t, s))
            def _():
                s1_copy(b, t, s).start()

            @pl.when(lat == owner(b, t, s))
            def _():
                r1_ref[b, t, lat] = strip_ref[b, t, s]

    def stage1_sent(b, t):
        for s in range(6):
            @pl.when(lat != owner(b, t, s))
            def _():
                s1_copy(b, t, s).wait_send()

    def wait_bytes(ref, sem):
        pltpu.make_async_copy(ref, ref, sem).wait()

    def stage1_reduce(b, t):
        mine, _ = owned(b, t)

        @pl.when(mine)
        def _():
            wait_bytes(r1_ref.at[b, t, pl.ds(0, NLAT - 1)], s1_recv.at[b, t])
            acc = r1_ref[b, t, 0].astype(F32)
            for i in range(1, NLAT):
                acc = acc + r1_ref[b, t, i].astype(F32)
            spread = nn(sel_ref[...], acc.astype(BF)).astype(BF)
            for j in range(NLON):
                s2_ref[b, t, j] = spread[16 * j:16 * j + 16]
            r2_ref[b, t, lon] = s2_ref[b, t, lon]

            def send(k, carry):
                to = at_lon(k)
                pltpu.make_async_remote_copy(
                    src_ref=s2_ref.at[b, t, to],
                    dst_ref=r2_ref.at[b, t, lon],
                    send_sem=s2_send.at[b, t],
                    recv_sem=s2_recv.at[b, t],
                    device_id={"lon": to},
                    device_id_type=MESH,
                ).start()
                return carry

            lax.fori_loop(1, NLON, send, 0)

    def stage2_reduce(b, t):
        mine, which = owned(b, t)

        @pl.when(mine)
        def _():
            wait_bytes(r2_ref.at[b, t, pl.ds(0, NLON - 1)], s2_recv.at[b, t])
            acc = r2_ref[b, t, 0].astype(F32)
            for i in range(1, NLON):
                acc = acc + r2_ref[b, t, i].astype(F32)
            total = acc.astype(BF)
            s3_ref[b, t] = total
            r3_ref[b, t, which] = total

            def send(k, carry):
                pltpu.make_async_remote_copy(
                    src_ref=s3_ref.at[b, t],
                    dst_ref=r3_ref.at[b, t, which],
                    send_sem=s3_send.at[b, t],
                    recv_sem=s3_recv.at[b, t],
                    device_id={"lat": at_lat(k)},
                    device_id_type=MESH,
                ).start()
                return carry

            lax.fori_loop(1, NLAT, send, 0)

    def stage3_finish(b, t):
        mine, _ = owned(b, t)

        @pl.when(mine)
        def _():
            wait_bytes(r3_ref.at[b, t, pl.ds(0, 5)], s3_recv.at[b, t])

        @pl.when(jnp.logical_not(mine))
        def _():
            wait_bytes(r3_ref.at[b, t], s3_recv.at[b, t])

        full = jnp.concatenate([r3_ref[b, t, s].astype(F32)[0:8] for s in range(6)], axis=1)
        if t == 0:
            for s in range(4):
                part = full[:, 192 * s:192 * s + 192]
                for i in range(SHARD):
                    odown_ref[b, 4 * i + s:4 * i + s + 1, :] = part[i:i + 1]
        elif t == 1:
            oup_ref[b] = full[0:SHARD]
        else:
            oqkv_ref[b] = full[0:SHARD, 0:576]
            oproj_ref[b] = full[0:SHARD, 576:768]

    def stages_sent(b, t):
        mine, _ = owned(b, t)
        stage1_sent(b, t)

        @pl.when(mine)
        def _():
            wait_bytes(s2_ref.at[b, t, pl.ds(0, NLON - 1)], s2_send.at[b, t])
            wait_bytes(s2_ref.at[b, t, pl.ds(0, NLAT - 1)], s3_send.at[b, t])

    tiles = (18, 12)
    tile0 = (0, 18)

    def fold_bias(b):
        total = None
        for c in range(WLON):
            if b == 0:
                spread = [onehot(iota((128, 384), 1) == key_target(TOK, 256, (256, 1), 0)[128 * t:128 * t + 128]) for t in range(2)]
                got = [ds1_ref[t, pl.ds(QPOS[c], 96, stride=16), :].astype(BF) for t in range(2)]
                part = nn(got[0], spread[0]) + nn(got[1][:, 0:64], spread[1][0:64])
            else:
                spread = [onehot(iota((128, 256), 1) == key_target(96, 128, (128, 1), 0))]
                got = ds2_ref[pl.ds(QPOS[c], 96, stride=16), :].astype(BF)
                part = nn(got[:, 0:96], spread[0][0:96])
            width = part.shape[1]
            if c:
                part = pltpu.roll(part, width - c, 1)
            total = part if total is None else total + part
        total = total.astype(BF)
        lanes = total.shape[1] // 128
        for rt in range(6):
            for lt in range(lanes):
                bs_ref[tile0[b] + rt * lanes + lt] = total[16 * rt:16 * rt + 16, 128 * lt:128 * lt + 128]

    def b_copy(b, i):
        return pltpu.make_async_remote_copy(
            src_ref=bs_ref.at[i],
            dst_ref=br_ref.at[lon],
            send_sem=b_send.at[i],
            recv_sem=b_recv,
            device_id={"lon": i},
            device_id_type=MESH,
        )

    def bias_send(b):
        for i in range(tile0[b], tile0[b] + tiles[b]):
            @pl.when(lon != i)
            def _():
                b_copy(b, i).start()

            @pl.when(lon == i)
            def _():
                br_ref[lon] = bs_ref[i]

    def bias_mine(b):
        return (lon >= tile0[b]) & (lon < tile0[b] + tiles[b])

    def bias_reduce(b):
        @pl.when(bias_mine(b))
        def _():
            wait_bytes(br_ref.at[pl.ds(0, NLON - 1)], b_recv)
            acc = br_ref[0].astype(F32)
            for i in range(1, NLON):
                acc = acc + br_ref[i].astype(F32)
            ball_ref[lon] = acc.astype(BF)

            def send(k, carry):
                pltpu.make_async_remote_copy(
                    src_ref=ball_ref.at[lon],
                    dst_ref=ball_ref.at[lon],
                    send_sem=bg_send,
                    recv_sem=bg_recv.at[b],
                    device_id={"lon": at_lon(k)},
                    device_id_type=MESH,
                ).start()
                return carry

            lax.fori_loop(1, NLON, send, 0)

    def bias_finish(b):
        mine = bias_mine(b)

        @pl.when(mine)
        def _():
            wait_bytes(ball_ref.at[pl.ds(tile0[b], tiles[b] - 1)], bg_recv.at[b])

        @pl.when(jnp.logical_not(mine))
        def _():
            wait_bytes(ball_ref.at[pl.ds(tile0[b], tiles[b])], bg_recv.at[b])

        lanes = 3 if b == 0 else 2
        for a in range(ZONES):
            row = jnp.concatenate(
                [
                    ball_ref[tile0[b] + (a // 2) * lanes + lt].astype(F32)[8 * (a % 2):8 * (a % 2) + 6]
                    for lt in range(lanes)
                ],
                axis=1,
            )
            if b == 0:
                obias_ref[b, :, TAB * a:TAB * a + TAB] = row[:, 0:TAB]
            else:
                half = row[:, 0:138]
                zero = jnp.zeros((6, 138), F32)
                both = [half, zero] if a < 6 else [zero, half]
                obias_ref[b, :, TAB * a:TAB * a + TAB] = jnp.concatenate(both, axis=1)

    def bias_sent(b):
        for i in range(tile0[b], tile0[b] + tiles[b]):
            @pl.when(lon != i)
            def _():
                b_copy(b, i).wait_send()

        @pl.when(bias_mine(b))
        def _():
            wait_bytes(br_ref.at[pl.ds(0, NLON - 1)], bg_send)

    expand_bias(0)
    u1 = load_window(x_ref)
    out1 = forward(0, u1)
    pl.semaphore_wait(barrier, NLAT - 1 + NLON - 1 + 2)
    exchange_start(1, out1)
    ct = load_window(ct_ref)
    exchange_start(0, ct)
    expand_bias(1)
    for s in range(4):
        perm_ref[192 * s:192 * s + 192, :] = onehot(iota((192, HID), 1) == 4 * iota((192, HID), 0) + s)
    row = iota((512, 1), 0)
    pos = row & 15
    sel_ref[...] = onehot(iota((512, C), 1) == jnp.where(pos < SHARD, (row >> 4) * SHARD + pos, -1))
    u2 = exchange_finish(1, out1)
    out2 = forward(1, u2)
    exchange_start(2, out2)
    g2 = exchange_finish(0, ct)
    ghid2 = backward_mlp(1, g2)
    gsec = backward_attention(1, ghid2)
    exchange_start(3, gsec)
    grads_mlp(1)
    grads_attention(1)
    for t in range(3):
        stage1_send(1, t)
    fold_bias(1)
    bias_send(1)
    store_window(res_ref, exchange_finish(2, out2))
    g1 = exchange_finish(3, gsec)
    ghid1 = backward_mlp(0, g1)
    grads_mlp(0)
    stage1_send(0, 0)
    stage1_send(0, 1)
    for t in range(3):
        stage1_reduce(1, t)
    bias_reduce(1)
    gin = backward_attention(0, ghid1)
    grads_attention(0)
    stage1_send(0, 2)
    fold_bias(0)
    bias_send(0)
    stage1_reduce(0, 0)
    stage1_reduce(0, 1)
    for t in range(3):
        stage2_reduce(1, t)
    store_window(gin_ref, gin)
    bias_finish(1)
    stage1_reduce(0, 2)
    bias_reduce(0)
    for t in range(3):
        stage3_finish(1, t)
    stage2_reduce(0, 0)
    stage2_reduce(0, 1)
    stage2_reduce(0, 2)
    bias_finish(0)
    for t in range(3):
        stage3_finish(0, t)
    for b in range(2):
        for t in range(3):
            stages_sent(b, t)
        bias_sent(b)


def on_device(inputs, cotangent, w_qkv, w_proj, w_up, w_down, earth_bias):
    vm = pl.BlockSpec(memory_space=pltpu.VMEM)
    outs = pl.pallas_call(
        kernel,
        out_shape=(
            jax.ShapeDtypeStruct((2, 6, 12, C), BF),
            jax.ShapeDtypeStruct((2, 6, 12, C), BF),
            jax.ShapeDtypeStruct((2, SHARD, 576), F32),
            jax.ShapeDtypeStruct((2, SHARD, 192), F32),
            jax.ShapeDtypeStruct((2, SHARD, 768), F32),
            jax.ShapeDtypeStruct((2, 24, 192), F32),
            jax.ShapeDtypeStruct((2, HEADS, 3312), F32),
        ),
        in_specs=[vm] * 7,
        out_specs=(vm,) * 7,
        scratch_shapes=[
            pltpu.VMEM((TOK, C), F32),
            pltpu.VMEM((2, TOK, C), BF),
            pltpu.VMEM((2, TOK, C), F32),
            pltpu.VMEM((2, TOK, 1), F32),
            pltpu.VMEM((2, TOK, 576), BF),
            pltpu.VMEM((HEADS, TOK, TOK), BF),
            pltpu.VMEM((HEADS, TOK, 96), BF),
            pltpu.VMEM((2, TOK, C), BF),
            pltpu.VMEM((2, TOK, C), F32),
            pltpu.VMEM((2, TOK, 1), F32),
            pltpu.VMEM((2, TOK, C), BF),
            pltpu.VMEM((2, TOK, HID), BF),
            pltpu.VMEM((2, TOK, HID), BF),
            pltpu.VMEM((2, TOK, HID), BF),
            pltpu.VMEM((2, TOK, 576), BF),
            pltpu.VMEM((2, TOK, C), BF),
            pltpu.VMEM((2, TOK, C), BF),
            pltpu.VMEM((96, 384), F32),
            pltpu.VMEM((2, 1536, 128), F32),
            pltpu.VMEM((1536, 128), F32),
            pltpu.VMEM((2, 1536, 128), F32),
            pltpu.VMEM((1536, 128), F32),
            pltpu.VMEM((HID, HID), BF),
            pltpu.VMEM((512, C), BF),
            pltpu.VMEM((4, 3, 48, C), BF),
            pltpu.VMEM((4, 3, 48, C), BF),
            pltpu.VMEM((2, 3, 6, C, 128), BF),
            pltpu.VMEM((2, 3, NLAT, C, 128), BF),
            pltpu.VMEM((2, 3, NLON, 16, 128), BF),
            pltpu.VMEM((2, 3, NLON, 16, 128), BF),
            pltpu.VMEM((2, 3, 16, 128), BF),
            pltpu.VMEM((2, 3, 6, 16, 128), BF),
            pltpu.VMEM((30, 16, 128), BF),
            pltpu.VMEM((NLON, 16, 128), BF),
            pltpu.VMEM((NLON, 16, 128), BF),
            pltpu.SemaphoreType.DMA((4, 3)),
            pltpu.SemaphoreType.DMA((4, 3)),
            pltpu.SemaphoreType.DMA((2, 3, 6)),
            pltpu.SemaphoreType.DMA((2, 3)),
            pltpu.SemaphoreType.DMA((2, 3)),
            pltpu.SemaphoreType.DMA((2, 3)),
            pltpu.SemaphoreType.DMA((2, 3)),
            pltpu.SemaphoreType.DMA((2, 3)),
            pltpu.SemaphoreType.DMA((30,)),
            pltpu.SemaphoreType.DMA,
            pltpu.SemaphoreType.DMA,
            pltpu.SemaphoreType.DMA((2,)),
        ],
        compiler_params=pltpu.CompilerParams(
            collective_id=0, has_side_effects=True, vmem_limit_bytes=50 * 1024 * 1024
        ),
        name="earth_blocks",
    )(inputs, cotangent, w_qkv, w_proj, w_up, w_down, earth_bias.reshape(2, HEADS, 3312))
    result, grad_inputs, g_qkv, g_proj, g_up, g_down, g_bias = outs
    return result, grad_inputs, g_qkv, g_proj, g_up, g_down, g_bias.reshape(2, 1, 1, HEADS, 3312)


def solution(mesh):
    field = P(None, "lat", "lon", None)
    shard = P(None, "lon", None)
    bias = P(None, "lat", None, None, None)
    return jax.shard_map(
        on_device,
        mesh=mesh,
        in_specs=(field, field, P(), P(), P(), P(), bias),
        out_specs=(field, field, shard, shard, shard, shard, bias),
        check_vma=False,
    )
```

time: 553 us -> 90.6 us (0.16)
  waiting for transfers between devices: 268 us -> 0 us
  Pallas kernels: 0 us -> 80.8 us
  blocking collectives: 70.8 us -> 0 us
  local copies, waits for them, and re-layouts: 72.5 us -> 7.95 us
  matrix products: 62.1 us -> 0 us
  starting transfers between devices: 35.9 us -> 0 us
  other arithmetic: 23.5 us -> 0 us
  between operations: 16.6 us -> 0.73 us
    unnamed x2 -> x0, waiting for transfers between devices: 261 us -> none
    pallas_call x0 -> x1, Pallas kernels: none -> 80.8 us  [on_device(): pl.pallas_call(kernel, out_shape=(jax.ShapeDtypeStruct((2, 6, 12, C), BF)...]
    psum x1 -> x0, blocking collectives: 70.8 us -> none  [on_device(): lax.psum(stacked[3].astype(jnp.bfloat16), 'lat').astype(jnp.float32)]
    dot_general x40 -> x0, matrix products: 62.1 us -> none  [the longest x28 30.7 us: product(): jnp.einsum(spec_text, left_side, right_side, preferred_element_type=jnp.f...]
    another operation x19 -> x0, local copies, waits for them, and re-layouts: 51.8 us -> none  [the longest x4 33.4 us: block_forward(): win_bias[:, :, None]]
    ppermute x8 -> x0, starting transfers between devices: 35.9 us -> none  [passed_along(): return lax.ppermute(value, axis, pairs)]
    convert_element_type x14 -> x0, local copies, waits for them, and re-layouts: 7.48 us -> none  [the longest x7 2.37 us: block_forward(): inputs_f = windows.astype(jnp.float32)]
    ppermute x8 -> x0, waiting for transfers between devices: 7.03 us -> none  [passed_along(): return lax.ppermute(value, axis, pairs)]
  transfers between devices with their start and end apart: 9 -> 0, of which waited for: 4 -> 0; matrix products, arithmetic and copies ran while one was open for 9% -> 0% of each run, Pallas kernels for 0% -> 0%
where the time goes in v1:
time: 90.6 us; the launch traced here: 89.5 us
  Pallas kernels  80.8 us (89%)
  local copies, waits for them, and re-layouts  7.95 us (9%)
    pallas_call x1, Pallas kernels, on_device(): pl.pallas_call(kernel, out_shape=(jax.ShapeDtypeStruct((2, 6, 12, C), BF)...  80.8 us
    unnamed x21, local copies, waits for them, and re-layouts  7.92 us

profile of v1, /device:TPU:1, one launch (start us, length us, event | category | flops | bytes accessed | tf_op | source)
XLA Modules:
  0.0 89.5 jit_solution(11772848732777852354)
XLA Ops:
  0.6 0.0 copy-start.4
  0.6 0.0 copy-start.3
  0.7 1.0 %copy.24.x_ref = bf16[2,6,12,192]{3,2,1,0:T(8,128)(2,1)S(1)} copy(bf16[2,6,12,192]{3,0,2,1:T(2,128)(2,1)} %param.7) | data formatting | bytes 110592 | tf_op args[0]
  1.6 0.9 %copy.25.ct_ref = bf16[2,6,12,192]{3,2,1,0:T(8,128)(2,1)S(1)} copy(bf16[2,6,12,192]{3,0,2,1:T(2,128)(2,1)} %param.8) | data formatting | bytes 110592 | tf_op args[1]
  2.5 0.0 copy-done.4
  2.5 0.1 copy.35
  2.7 0.0 copy-done.3
  2.7 0.0 copy-start
  2.7 0.0 copy-start.1
  2.7 0.0 copy-start.2
  2.7 0.3 copy.26.wdown_ref
  3.0 0.8 copy-done
  3.7 0.1 copy-done.1
  3.9 0.0 copy-done.2
  3.9 80.8 %earth_blocks.1 = (bf16[2,6,12,192]{3,2,1,0:T(8,128)(2,1)S(1)}, bf16[2,6,12,192]{3,2,1,0:T(8,128)(2,1)S(1)}, f32[2,6,576]{2,1,0:T(8,128)S(1)}, f32[2,6,192]{2,1,...) custom-call(bf16[2,6,12,192]{3,2,1,0:T(8,128)(2,1)S(1)} %copy.24.x_ref, ...), custom_call_target="tpu_custom_call" | custom-call | tf_op jit(solution)/shard_map/earth_blocks/pallas_call | solution.py:679
  84.8 0.7 copy.28
  85.5 0.6 copy.31
  86.1 0.6 copy.30
  86.7 0.6 copy.32
  87.3 0.7 copy.29
  88.0 0.8 copy.33
  88.9 0.6 copy.37
  (1 shorter events, 0.0 us)
Async XLA Ops:
  0.6 1.9 %copy-start.4 = (f32[2,1,1,6,3312]{4,2,3,1,0:T(1,128)S(1)}, f32[2,1,1,6,3312]{4,2,3,1,0:T(1,128)}, u32[]{:S(2)}) copy-start(f32[2,1,1,6,3312]{4,2,3,1,0:T(1,128)} %param.13) | copy-start | bytes 476932
  0.6 2.0 %copy-start.3 = (bf16[2,768,192]{1,2,0:T(8,128)(2,1)S(1)}, bf16[2,768,192]{1,2,0:T(8,128)(2,1)}, u32[]{:S(2)}) copy-start(bf16[2,768,192]{1,2,0:T(8,128)(2,1)} %param.12) | copy-start | bytes 1769476
  2.7 1.1 %copy-start = (bf16[2,192,768]{2,1,0:T(8,128)(2,1)S(1)}, bf16[2,192,768]{2,1,0:T(8,128)(2,1)}, u32[]{:S(2)}) copy-start(bf16[2,192,768]{2,1,0:T(8,128)(2,1)} %wup_ref.1) | copy-start | bytes 1769476
  2.7 1.2 %copy-start.1 = (bf16[2,192,576]{2,1,0:T(8,128)(2,1)S(1)}, bf16[2,192,576]{2,1,0:T(8,128)(2,1)}, u32[]{:S(2)}) copy-start(bf16[2,192,576]{2,1,0:T(8,128)(2,1)} %wqkv_ref.1) | copy-start | bytes 1327108
  2.7 1.2 %copy-start.2 = (bf16[2,192,192]{2,1,0:T(8,128)(2,1)S(1)}, bf16[2,192,192]{2,1,0:T(8,128)(2,1)}, u32[]{:S(2)}) copy-start(bf16[2,192,192]{2,1,0:T(8,128)(2,1)} %wproj_ref.1) | copy-start | bytes 442372

commit v2 on v1

v2 whole, which is shorter than its diff:
```python
import jax
import jax.numpy as jnp
from jax import lax
from jax.experimental import pallas as pl
from jax.experimental.pallas import tpu as pltpu
from jax.sharding import PartitionSpec as P

BF = jnp.bfloat16
F32 = jnp.float32
MESH = pl.DeviceIdType.MESH

HEADS = 6
C = 192
HID = 768
WLON = 12
ZONES = 12
REACH = 23
TAB = ZONES * REACH
NLAT = 16
NLON = 32
RING = 16
CHIPS = 8
SHARD = 6
TOK = 192
NEG_FILL = -1e30
LN_EPS = 1e-05
SCALE = 32.0 ** -0.5
NORM = 73728.0 ** -0.5

QPOS = [c if c < 6 else c + 2 for c in range(WLON)]
PAD_POS = [6, 7, 14, 15]


def nn(a, b):
    return lax.dot_general(a, b, (((1,), (0,)), ((), ())), preferred_element_type=F32)


def nt(a, b):
    return lax.dot_general(a, b, (((1,), (1,)), ((), ())), preferred_element_type=F32)


def iota(shape, dim):
    return lax.broadcasted_iota(jnp.int32, shape, dim)


def onehot(cond):
    return jnp.where(cond, 1.0, 0.0).astype(BF)


def ln(x):
    mean = jnp.mean(x, axis=-1, keepdims=True)
    centred = x - mean
    inv = lax.rsqrt(jnp.mean(centred * centred, axis=-1, keepdims=True) + LN_EPS)
    return centred * inv, inv


def ln_back(scaled, inv, grad):
    mean_grad = jnp.mean(grad, axis=-1, keepdims=True)
    mean_proj = jnp.mean(grad * scaled, axis=-1, keepdims=True)
    return inv * (grad - mean_grad - scaled * mean_proj)


def gelu_pair(v):
    gauss = jnp.exp(-0.5 * v * v)
    t = 1.0 / (1.0 + (0.3275911 * 0.7071067811865476) * jnp.abs(v))
    poly = t * (
        0.127414796 + t * (-0.142248368 + t * (0.7107068705 + t * (-0.7265760135 + t * 0.5307027145)))
    )
    tail = poly * gauss
    phi = jnp.where(v < 0.0, tail, 1.0 - tail)
    return v * phi, phi + v * gauss * 0.3989422804014327


def key_target(lanes, width, shape, dim):
    y = iota(shape, dim)
    pos = y & 15
    col = jnp.where(pos < 8, pos, pos - 2)
    valid = ((pos & 7) < 6) & (y < lanes)
    return jnp.where(valid, (y >> 4) * REACH + col + (WLON - 1), -1)


def kernel(
    x_ref, ct_hbm, wqkv_hbm, wproj_hbm, wup_hbm, wdown_hbm, eb_ref,
    res_ref, gin_ref, oqkv_ref, oproj_ref, oup_ref, odown_ref, obias_ref,
    ct_ref, wqkv_ref, wproj_ref, wup_ref, wdown_ref, in_sem, win_ref, n1_ref, sc1_ref, inv1_ref, qkv_ref, p1_ref, p2_ref, mix_ref, sc2_ref, inv2_ref, n2_ref,
    act_ref, slope_ref, gpre_ref, gqkv_ref, ghb_ref, g_ref,
    t_ref, bias1_ref, bias2_ref, ds1_ref, ds2_ref,
    perm_ref, sel_ref,
    xs_ref, xr_ref,
    strip_ref, r0_ref, a_du_ref, a_qp_ref, r1_du_ref, r1_qp_ref, s2_ref, r2_ref, s3_ref, r3_ref,
    bs_ref, br_ref, ball_ref,
    x_send, x_recv, s0_send, s0_recv, s1_send, s1_recv, s2_send, s2_recv, s3_send, s3_recv,
    b_send, b_recv, bg_send, bg_recv,
):
    lat = lax.axis_index("lat")
    lon = lax.axis_index("lon")

    def at_lat(k):
        return lax.rem(lat + k + NLAT, NLAT)

    def at_lon(k):
        return lax.rem(lon + k + NLON, NLON)

    loads = [
        pltpu.make_async_copy(src, dst, in_sem.at[i])
        for i, (src, dst) in enumerate(
            (
                (wqkv_hbm, wqkv_ref),
                (wproj_hbm, wproj_ref),
                (wup_hbm, wup_ref),
                (wdown_hbm, wdown_ref),
                (ct_hbm, ct_ref),
            )
        )
    ]
    for load in loads:
        load.start()

    barrier = pltpu.get_barrier_semaphore()

    def greet_lat(k, carry):
        pl.semaphore_signal(barrier, inc=1, device_id={"lat": at_lat(k)}, device_id_type=MESH)
        return carry

    def greet_lon(k, carry):
        pl.semaphore_signal(barrier, inc=1, device_id={"lon": at_lon(k)}, device_id_type=MESH)
        return carry

    lax.fori_loop(1, NLAT, greet_lat, 0)
    lax.fori_loop(1, NLON, greet_lon, 0)
    def greet_far(k, carry):
        to = {"lat": lax.rem(lat + 2 * k, NLAT), "lon": lax.rem(lon + RING, NLON)}
        pl.semaphore_signal(barrier, inc=1, device_id=to, device_id_type=MESH)
        return carry

    lax.fori_loop(1, CHIPS, greet_far, 0)
    for k in (-1, 1):
        pl.semaphore_signal(
            barrier, inc=1, device_id={"lat": at_lat(k), "lon": at_lon(k)}, device_id_type=MESH
        )

    lane = iota((1, C), 1) >> 5
    hm = [onehot(lane == h) for h in range(HEADS)]
    eye = onehot(iota((C, C), 0) == iota((C, C), 1))
    tgt1 = key_target(TOK, 256, (1, 256), 1)
    tgt2 = key_target(96, 128, (1, 128), 1)

    def load_window(src):
        win_ref[...] = jnp.zeros((TOK, C), F32)
        for r in range(6):
            for c in range(WLON):
                v = src[r, c].astype(F32)
                for lev in range(2):
                    at = 96 * lev + 16 * r + QPOS[c]
                    win_ref[at:at + 1, :] = v[lev:lev + 1]
        return win_ref[...]

    def store_window(dst, val):
        for r in range(6):
            for c in range(WLON):
                at = 16 * r + QPOS[c]
                dst[r, c] = jnp.concatenate([val[at:at + 1], val[at + 96:at + 97]], axis=0).astype(BF)

    def group(val, lev, row, half):
        at = 96 * lev + 16 * row + 8 * half
        return val[at:at + 8]

    def strip(val, row0, half):
        return jnp.concatenate(
            [group(val, lev, row0 + r, half) for lev in range(2) for r in range(3)], axis=0
        ).astype(BF)

    def exchange_copies(idx):
        step = -1 if idx < 2 else 1
        targets = (
            {"lon": at_lon(step)},
            {"lat": at_lat(step)},
            {"lat": at_lat(step), "lon": at_lon(step)},
        )
        return [
            pltpu.make_async_remote_copy(
                src_ref=xs_ref.at[idx, i],
                dst_ref=xr_ref.at[idx, i],
                send_sem=x_send.at[idx, i],
                recv_sem=x_recv.at[idx, i],
                device_id=targets[i],
                device_id_type=MESH,
            )
            for i in range(3)
        ]

    def exchange_start(idx, val):
        if idx < 2:
            parts = (strip(val, 3, 0), strip(val, 0, 1), strip(val, 0, 0))
        else:
            parts = (strip(val, 0, 1), strip(val, 3, 0), strip(val, 3, 1))
        for i, copy in enumerate(exchange_copies(idx)):
            xs_ref[idx, i] = parts[i]
            copy.start()

    def exchange_finish(idx, val):
        for copy in exchange_copies(idx):
            copy.wait()
        got = [xr_ref[idx, i].astype(F32) for i in range(3)]
        row_near = 0 if idx < 2 else 3
        half_near = 0 if idx < 2 else 1
        rows = []
        for lev in range(2):
            old = 1 - lev
            for row in range(6):
                near_row = (row < 3) == (row_near == 0)
                r = row % 3
                pieces = []
                for half in range(2):
                    near_half = half == half_near
                    at = 24 * old + 8 * r
                    if near_row and near_half:
                        piece = group(val, old, (3 if idx < 2 else 0) + r, 1 - half)
                    elif near_row:
                        piece = got[0][at:at + 8]
                    elif near_half:
                        piece = got[1][at:at + 8]
                    else:
                        piece = got[2][at:at + 8]
                    pieces.append(piece)
                rows += pieces
        return jnp.concatenate(rows, axis=0)

    def load_table(b):
        t_ref[...] = jnp.zeros_like(t_ref)
        for a in range(ZONES):
            if b == 0:
                rows = pl.ds(a, HEADS, stride=ZONES)
            else:
                rows = pl.ds(36 * (a // 6) + a % 6, HEADS, stride=6)
            for lt in range(3):
                width = min(128, TAB - 128 * lt)
                lane = TAB * a + 128 * lt
                piece = eb_ref[b, :, lane:lane + width]
                if width < 128:
                    piece = jnp.concatenate([piece, jnp.zeros((HEADS, 128 - width), F32)], axis=1)
                t_ref[lt, rows, :] = piece
        return jnp.concatenate([t_ref[lt] for lt in range(3)], axis=1)

    def split3(v):
        hi = v.astype(BF)
        rest = v - hi.astype(F32)
        mid = rest.astype(BF)
        return hi, mid, (rest - mid.astype(F32)).astype(BF)

    def expand_bias(b):
        table = load_table(b)
        if b == 0:
            spread = onehot(iota((384, 256), 0) == tgt1)
            mask = jnp.broadcast_to(jnp.where(tgt1 < 0, NEG_FILL, 0.0), (72, 256))
        else:
            spread = jnp.concatenate(
                [onehot(iota((384, 128), 0) == jnp.where(tgt2 < 0, -1, tgt2 + 138 * lv)) for lv in range(2)], axis=1
            )
            row = iota((72, 1), 0)
            row = jnp.where(row >= 36, row - 36, row)
            far_row = jnp.where(lax.rem(row, 6) >= 3, 1, 0)
            far_key = jnp.where(iota((1, 128), 1) >= 48, 1, 0)
            last = jnp.where(lat == NLAT - 1, 1, 0)
            cut = (far_row + far_key) * last == 1
            mask = jnp.where(cut | (tgt2 < 0), NEG_FILL, 0.0)
            low = iota((72, 1), 0) < 36
        for c in range(WLON):
            rolled = pltpu.roll(table, c, 1) if c else table
            full = sum(nn(p, spread) for p in split3(rolled))
            if b == 0:
                full = full + mask
                for t in range(2):
                    bias1_ref[t, pl.ds(QPOS[c], 72, stride=16), :] = full[:, 128 * t:128 * t + 128]
            else:
                bias2_ref[pl.ds(QPOS[c], 72, stride=16), :] = jnp.where(low, full[:, 0:128], full[:, 128:256]) + mask
        for p in PAD_POS:
            if b == 0:
                for t in range(2):
                    bias1_ref[t, pl.ds(p, 72, stride=16), :] = mask[:, 128 * t:128 * t + 128]
            else:
                bias2_ref[pl.ds(p, 72, stride=16), :] = mask

    def head_bias(b, h, seg):
        if b == 0:
            rows = slice(TOK * h, TOK * h + TOK)
            return jnp.concatenate([bias1_ref[0, rows, :], bias1_ref[1, rows, 0:64]], axis=1)
        at = 96 * (HEADS * seg + h)
        return bias2_ref[at:at + 96, 0:96]

    segments = ((0, TOK),), ((0, 96), (96, 96))

    def forward(b, u):
        sc1, inv1 = ln(u)
        n1 = sc1.astype(BF)
        n1_ref[b] = n1
        sc1_ref[b] = sc1
        inv1_ref[b] = inv1
        qkv_ref[b] = nn(n1, wqkv_ref[b]).astype(BF)
        for seg, (start, size) in enumerate(segments[b]):
            q = qkv_ref[b, start:start + size, 0:C]
            k = qkv_ref[b, start:start + size, C:2 * C]
            v = qkv_ref[b, start:start + size, 2 * C:3 * C]
            mixed = jnp.zeros((size, C), F32)
            for h in range(HEADS):
                scores = nt(q * hm[h], k) * SCALE + head_bias(b, h, seg)
                top = jnp.max(scores, axis=-1, keepdims=True)
                e = jnp.exp(scores - top)
                probs = (e * (1.0 / jnp.sum(e, axis=-1, keepdims=True))).astype(BF)
                if b == 0:
                    p1_ref[h] = probs
                else:
                    p2_ref[h, start:start + size, :] = probs
                mixed = mixed + nn(probs, v * hm[h])
            mix_ref[b, start:start + size, :] = mixed.astype(BF)
        hidden = (u + nn(mix_ref[b], wproj_ref[b])).astype(BF).astype(F32)
        sc2, inv2 = ln(hidden)
        n2 = sc2.astype(BF)
        sc2_ref[b] = sc2
        inv2_ref[b] = inv2
        n2_ref[b] = n2
        acc = hidden
        for c in range(0, HID, 256):
            act, slope = gelu_pair(nn(n2, wup_ref[b, :, c:c + 256]))
            act = act.astype(BF)
            act_ref[b, :, c:c + 256] = act
            slope_ref[b, :, c:c + 256] = slope.astype(BF)
            acc = acc + nt(act, wdown_ref[b, :, c:c + 256])
        return acc.astype(BF).astype(F32)

    def backward_mlp(b, gf):
        g = gf.astype(BF)
        g_ref[b] = g
        gn2 = jnp.zeros((TOK, C), F32)
        for c in range(0, HID, 256):
            gact = nn(g, wdown_ref[b, :, c:c + 256])
            gpre = (gact * slope_ref[b, :, c:c + 256].astype(F32)).astype(BF)
            gpre_ref[b, :, c:c + 256] = gpre
            gn2 = gn2 + nt(gpre, wup_ref[b, :, c:c + 256])
        ghid = gf + ln_back(sc2_ref[b], inv2_ref[b], gn2)
        ghb_ref[b] = ghid.astype(BF)
        return ghid

    def attention_grads(b):
        gmix_all = nt(ghb_ref[b], wproj_ref[b]).astype(BF)
        for seg, (start, size) in enumerate(segments[b]):
            rows = slice(start, start + size)
            q = qkv_ref[b, rows, 0:C]
            k = qkv_ref[b, rows, C:2 * C]
            v = qkv_ref[b, rows, 2 * C:3 * C]
            gmix = gmix_all[rows]
            qt = nt(eye, q).astype(BF)
            gmt = nt(eye, gmix).astype(BF)
            gq = jnp.zeros((size, C), F32)
            gkt = []
            gvt = []
            for h in range(HEADS):
                pb = p1_ref[h] if b == 0 else p2_ref[h, rows, :]
                pf = pb.astype(F32)
                gp = nt(gmix * hm[h], v)
                ds = pf * (gp - jnp.sum(gp * pf, axis=-1, keepdims=True))
                if b == 0:
                    ds1_ref[0, TOK * h:TOK * h + TOK, :] = ds[:, 0:128]
                    ds1_ref[1, TOK * h:TOK * h + TOK, 0:64] = ds[:, 128:192]
                else:
                    at = 96 * (HEADS * seg + h)
                    ds2_ref[at:at + 96, 0:96] = ds
                dsb = ds.astype(BF)
                gq = gq + nn(dsb, k * hm[h])
                gkt.append(nn(qt[32 * h:32 * h + 32], dsb))
                gvt.append(nn(gmt[32 * h:32 * h + 32], pb))
            small = eye if size == C else eye[0:size, 0:size]
            gk = nt(small, (jnp.concatenate(gkt, axis=0) * SCALE).astype(BF)).astype(BF)
            gv = nt(small, jnp.concatenate(gvt, axis=0).astype(BF)).astype(BF)
            gqkv_ref[b, rows, 0:C] = (gq * SCALE).astype(BF)
            gqkv_ref[b, rows, C:2 * C] = gk
            gqkv_ref[b, rows, 2 * C:3 * C] = gv

    def input_grad(b, ghid):
        gn1 = nt(gqkv_ref[b], wqkv_ref[b])
        return (ghid + ln_back(sc1_ref[b], inv1_ref[b], gn1)).astype(BF).astype(F32)

    def put_strips(b, t, s, val):
        val = (val * NORM).astype(BF)
        for i in range(val.shape[1] // 128):
            strip_ref[b, t, s + i] = val[:, 128 * i:128 * i + 128]

    def grads_mlp(b):
        actt = nt(perm_ref[...], act_ref[b]).astype(BF)
        g = g_ref[b]
        for pair in range(2):
            at = 384 * pair
            both = [nn(actt[at + 192 * i:at + 192 * i + 192], g) for i in range(2)]
            put_strips(b, 0, 3 * pair, jnp.concatenate(both, axis=1))
        n2t = nt(eye, n2_ref[b]).astype(BF)
        for s in range(3):
            put_strips(b, 1, 2 * s, nn(n2t, gpre_ref[b, :, 256 * s:256 * s + 256]))

    def grads_attention(b):
        n1t = nt(eye, n1_ref[b]).astype(BF)
        mixt = nt(eye, mix_ref[b]).astype(BF)
        put_strips(b, 2, 0, nn(n1t, gqkv_ref[b, :, 0:256]))
        put_strips(b, 2, 2, nn(n1t, gqkv_ref[b, :, 256:512]))
        rest = [nn(n1t, gqkv_ref[b, :, 512:576]), nn(mixt, ghb_ref[b])]
        put_strips(b, 2, 4, jnp.concatenate(rest, axis=1))

    core = lax.rem(lat, 2)
    chip = lat // 2
    ring = lon // RING
    z = lax.rem(lon, RING)
    half = C // 2
    a_refs = (a_du_ref, a_qp_ref)
    r1_refs = (r1_du_ref, r1_qp_ref)

    def place(b):
        return chip if b else lax.rem(chip + 4, 8)

    def owned(b, kind):
        at = place(b)
        if kind == 0:
            return at // 3 == core, at - 3 * core
        return (at >= 6) | (at == 3 - 3 * core), jnp.where(at >= 6, at - 6, 2)

    def owner(b, kind, i):
        if kind == 0:
            at = 3 * core + i
        else:
            at = 6 + i if i < 2 else 3 - 3 * core
        at = at if b else lax.rem(at + 4, 8)
        return 2 * at + core

    def wait_bytes(ref, sem):
        pltpu.make_async_copy(ref, ref, sem).wait()

    def s0_copy(b, t):
        return pltpu.make_async_remote_copy(
            src_ref=strip_ref.at[b, t, pl.ds(3 - 3 * core, 3)],
            dst_ref=r0_ref.at[b, t],
            send_sem=s0_send.at[b, t],
            recv_sem=s0_recv.at[b, t],
            device_id={"lat": lat + 1 - 2 * core},
            device_id_type=MESH,
        )

    def stage0_send(b, t):
        s0_copy(b, t).start()

    def s1_copy(b, kind, i, g):
        return pltpu.make_async_remote_copy(
            src_ref=a_refs[kind].at[b, i, g],
            dst_ref=r1_refs[kind].at[b, CHIPS * ring + chip],
            send_sem=s1_send.at[b, kind, i, g],
            recv_sem=s1_recv.at[b, kind],
            device_id={"lat": owner(b, kind, i), "lon": RING * g + z},
            device_id_type=MESH,
        )

    def s1_here(b, kind, i, g):
        return (lat == owner(b, kind, i)) & (ring == g)

    def stage1_send(b, kind):
        groups = (0, 1) if kind == 0 else (2,)
        for t in groups:
            s0_copy(b, t).wait_recv()
        for i in range(3):
            for part, t in enumerate(groups):
                both = strip_ref[b, t, 3 * core + i].astype(F32) + r0_ref[b, t, i].astype(F32)
                for g in range(2):
                    a_refs[kind][b, i, g, part] = both[half * g:half * g + half].astype(BF)
            for g in range(2):
                here = s1_here(b, kind, i, g)

                @pl.when(jnp.logical_not(here))
                def _():
                    s1_copy(b, kind, i, g).start()

                @pl.when(here)
                def _():
                    r1_refs[kind][b, CHIPS * ring + chip] = a_refs[kind][b, i, g]

    def stage1_reduce(b, kind):
        mine, _ = owned(b, kind)
        parts = 2 if kind == 0 else 1

        @pl.when(mine)
        def _():
            ref = r1_refs[kind]
            wait_bytes(ref.at[b, pl.ds(0, 2 * CHIPS - 1)], s1_recv.at[b, kind])
            spread = []
            for part in range(parts):
                acc = ref[b, 0, part].astype(F32)
                for i in range(1, 2 * CHIPS):
                    acc = acc + ref[b, i, part].astype(F32)
                spread.append(nn(sel_ref[...], acc.astype(BF)))
            if parts == 1:
                spread.append(jnp.zeros((8 * RING, 128), F32))
            for j in range(RING):
                tile = jnp.concatenate([v[8 * j:8 * j + 8] for v in spread], axis=0)
                s2_ref[b, kind, j] = tile.astype(BF)
            r2_ref[b, kind, z] = s2_ref[b, kind, z]

            def send(k, carry):
                to = lax.rem(z + k, RING)
                pltpu.make_async_remote_copy(
                    src_ref=s2_ref.at[b, kind, to],
                    dst_ref=r2_ref.at[b, kind, z],
                    send_sem=s2_send.at[b, kind],
                    recv_sem=s2_recv.at[b, kind],
                    device_id={"lon": RING * ring + to},
                    device_id_type=MESH,
                ).start()
                return carry

            lax.fori_loop(1, RING, send, 0)

    def stage2_reduce(b, kind):
        mine, i = owned(b, kind)
        which = 3 * core + i

        @pl.when(mine)
        def _():
            wait_bytes(r2_ref.at[b, kind, pl.ds(0, RING - 1)], s2_recv.at[b, kind])
            acc = r2_ref[b, kind, 0].astype(F32)
            for j in range(1, RING):
                acc = acc + r2_ref[b, kind, j].astype(F32)
            total = acc.astype(BF)
            s3_ref[b, kind] = total
            r3_ref[b, kind, which] = total

            def send(k, carry):
                pltpu.make_async_remote_copy(
                    src_ref=s3_ref.at[b, kind],
                    dst_ref=r3_ref.at[b, kind, which],
                    send_sem=s3_send.at[b, kind],
                    recv_sem=s3_recv.at[b, kind],
                    device_id={"lat": at_lat(k)},
                    device_id_type=MESH,
                ).start()
                return carry

            lax.fori_loop(1, NLAT, send, 0)

    def put_rows(ref, b, val):
        for i in range(SHARD):
            ref[i, b:b + 1, :] = val[i:i + 1]

    def stage3_finish(b, kind):
        mine, _ = owned(b, kind)

        @pl.when(mine)
        def _():
            wait_bytes(r3_ref.at[b, kind, pl.ds(0, 5)], s3_recv.at[b, kind])

        @pl.when(jnp.logical_not(mine))
        def _():
            wait_bytes(r3_ref.at[b, kind], s3_recv.at[b, kind])

        tiles = [r3_ref[b, kind, s].astype(F32) for s in range(6)]
        first = jnp.concatenate([v[0:8] for v in tiles], axis=1)
        if kind == 0:
            for s in range(4):
                part = first[:, 192 * s:192 * s + 192]
                for i in range(SHARD):
                    odown_ref[b, 4 * i + s:4 * i + s + 1, :] = part[i:i + 1]
            put_rows(oup_ref, b, jnp.concatenate([v[8:16] for v in tiles], axis=1))
        else:
            put_rows(oqkv_ref, b, first[:, 0:576])
            put_rows(oproj_ref, b, first[:, 576:768])

    def stages_sent(b):
        for t in range(3):
            s0_copy(b, t).wait_send()
        for kind in range(2):
            for i in range(3):
                for g in range(2):
                    @pl.when(jnp.logical_not(s1_here(b, kind, i, g)))
                    def _():
                        s1_copy(b, kind, i, g).wait_send()

            @pl.when(owned(b, kind)[0])
            def _():
                wait_bytes(s2_ref.at[b, kind, pl.ds(0, RING - 1)], s2_send.at[b, kind])
                wait_bytes(s2_ref.at[b, kind, pl.ds(0, NLAT - 1)], s3_send.at[b, kind])

    tiles = (11, 6)
    tile0 = (0, 11)

    def bias_home(b, i):
        return RING * (i % 2) + 3 * (i // 2) + b

    def bias_mine(b):
        i = 2 * (z // 3) + ring
        return (lax.rem(z, 3) == b) & (i < tiles[b]), i

    def fold_bias(b):
        total = None
        width = 384 if b == 0 else 256
        if b == 0:
            spread = onehot(iota((C, 384), 1) == key_target(TOK, 256, (C, 1), 0))
        else:
            spread = onehot(iota((96, 256), 1) == key_target(96, 128, (96, 1), 0))
        for c in range(WLON):
            if b == 0:
                got = [ds1_ref[t, pl.ds(QPOS[c], 72, stride=16), :].astype(BF) for t in range(2)]
                part = nn(got[0], spread[0:128]) + nn(got[1][:, 0:64], spread[128:C])
            else:
                part = nn(ds2_ref[pl.ds(QPOS[c], 72, stride=16), :].astype(BF)[:, 0:96], spread)
            if c:
                part = pltpu.roll(part, width - c, 1)
            total = part if total is None else total + part
        total = jnp.concatenate([total, jnp.zeros((8, width), F32)], axis=0)
        lanes = width // 128 - 1
        extra = TAB - 256 if b == 0 else 138 - 128
        for rt in range(5):
            for lt in range(lanes):
                tile = total[16 * rt:16 * rt + 16, 128 * lt:128 * lt + 128]
                bs_ref[tile0[b] + rt * lanes + lt] = tile.astype(BF)
        packed = None
        for rt in range(5):
            tile = total[16 * rt:16 * rt + 16, 128 * lanes:]
            if rt:
                tile = pltpu.roll(tile, extra * rt, 1)
                packed = jnp.where(iota((16, 128), 1) >= extra * rt, tile, packed)
            else:
                packed = tile
        bs_ref[tile0[b] + 5 * lanes] = packed.astype(BF)

    def b_copy(b, i):
        return pltpu.make_async_remote_copy(
            src_ref=bs_ref.at[tile0[b] + i],
            dst_ref=br_ref.at[lon],
            send_sem=b_send.at[tile0[b] + i],
            recv_sem=b_recv,
            device_id={"lon": bias_home(b, i)},
            device_id_type=MESH,
        )

    def bias_send(b):
        for i in range(tiles[b]):
            @pl.when(lon != bias_home(b, i))
            def _():
                b_copy(b, i).start()

            @pl.when(lon == bias_home(b, i))
            def _():
                br_ref[lon] = bs_ref[tile0[b] + i]

    def bias_reduce(b):
        mine, i = bias_mine(b)
        at = tile0[b] + i

        @pl.when(mine)
        def _():
            wait_bytes(br_ref.at[pl.ds(0, NLON - 1)], b_recv)
            acc = br_ref[0].astype(F32)
            for j in range(1, NLON):
                acc = acc + br_ref[j].astype(F32)
            ball_ref[at] = acc.astype(BF)

            def send(k, carry):
                pltpu.make_async_remote_copy(
                    src_ref=ball_ref.at[at],
                    dst_ref=ball_ref.at[at],
                    send_sem=bg_send,
                    recv_sem=bg_recv.at[b],
                    device_id={"lon": at_lon(k)},
                    device_id_type=MESH,
                ).start()
                return carry

            lax.fori_loop(1, NLON, send, 0)

    def bias_finish(b):
        mine, _ = bias_mine(b)

        @pl.when(mine)
        def _():
            wait_bytes(ball_ref.at[pl.ds(tile0[b], tiles[b] - 1)], bg_recv.at[b])

        @pl.when(jnp.logical_not(mine))
        def _():
            wait_bytes(ball_ref.at[pl.ds(tile0[b], tiles[b])], bg_recv.at[b])

        lanes = 2 if b == 0 else 1
        extra = TAB - 256 if b == 0 else 138 - 128
        packed = ball_ref[tile0[b] + 5 * lanes].astype(F32)
        for rt in range(5):
            rows = [ball_ref[tile0[b] + rt * lanes + lt].astype(F32) for lt in range(lanes)]
            rows.append(pltpu.roll(packed, 128 - extra * rt, 1) if rt else packed)
            for i in range(16 if rt < 4 else 8):
                at = 16 * rt + i
                if b == 0:
                    h, a = at // ZONES, at % ZONES
                    for lt in range(3):
                        width = min(128, TAB - 128 * lt)
                        lane = TAB * a + 128 * lt
                        obias_ref[0, h, :, lane:lane + width] = rows[lt][i:i + 1, 0:width]
                else:
                    level, h, a = at // 36, at % 36 // 6, at // 36 * 6 + at % 6
                    for lt in range(2):
                        width = min(128, 138 - 128 * lt)
                        lane = TAB * a + 138 * level + 128 * lt
                        obias_ref[1, h, :, lane:lane + width] = rows[lt][i:i + 1, 0:width]

    def bias_sent(b):
        for i in range(tiles[b]):
            @pl.when(lon != bias_home(b, i))
            def _():
                b_copy(b, i).wait_send()

        @pl.when(bias_mine(b)[0])
        def _():
            wait_bytes(br_ref.at[pl.ds(0, NLON - 1)], bg_send)

    expand_bias(0)
    u1 = load_window(x_ref)
    for load in loads[:4]:
        load.wait()
    out1 = forward(0, u1)
    pl.semaphore_wait(barrier, NLAT - 1 + NLON - 1 + CHIPS - 1 + 2)
    exchange_start(1, out1)
    loads[4].wait()
    ct = load_window(ct_ref)
    exchange_start(0, ct)
    expand_bias(1)
    for s in range(4):
        perm_ref[192 * s:192 * s + 192, :] = onehot(iota((192, HID), 1) == 4 * iota((192, HID), 0) + s)
    row = iota((8 * RING, 1), 0)
    pos = row & 7
    sel_ref[...] = onehot(iota((8 * RING, C // 2), 1) == jnp.where(pos < SHARD, (row >> 3) * SHARD + pos, -1))
    obias_ref[1] = jnp.zeros((HEADS, 1, ZONES * TAB), F32)
    u2 = exchange_finish(1, out1)
    out2 = forward(1, u2)
    exchange_start(2, out2)
    g2 = exchange_finish(0, ct)
    ghid2 = backward_mlp(1, g2)
    attention_grads(1)
    gsec = input_grad(1, ghid2)
    exchange_start(3, gsec)
    grads_mlp(1)
    stage0_send(1, 0)
    stage0_send(1, 1)
    grads_attention(1)
    stage0_send(1, 2)
    fold_bias(1)
    bias_send(1)
    stage1_send(1, 0)
    stage1_send(1, 1)
    store_window(res_ref, exchange_finish(2, out2))
    g1 = exchange_finish(3, gsec)
    ghid1 = backward_mlp(0, g1)
    grads_mlp(0)
    stage0_send(0, 0)
    stage0_send(0, 1)
    attention_grads(0)
    fold_bias(0)
    bias_send(0)
    grads_attention(0)
    stage0_send(0, 2)
    stage1_send(0, 0)
    stage1_reduce(1, 0)
    stage1_reduce(1, 1)
    stage1_send(0, 1)
    bias_reduce(1)
    store_window(gin_ref, input_grad(0, ghid1))
    stage1_reduce(0, 0)
    stage1_reduce(0, 1)
    bias_reduce(0)
    stage2_reduce(1, 0)
    stage2_reduce(1, 1)
    bias_finish(1)
    stage2_reduce(0, 0)
    stage2_reduce(0, 1)
    stage3_finish(1, 0)
    stage3_finish(1, 1)
    bias_finish(0)
    stage3_finish(0, 0)
    stage3_finish(0, 1)
    for b in range(2):
        stages_sent(b)
        bias_sent(b)


def on_device(inputs, cotangent, w_qkv, w_proj, w_up, w_down, earth_bias):
    vm = pl.BlockSpec(memory_space=pltpu.VMEM)
    hbm = pl.BlockSpec(memory_space=pltpu.HBM)
    shapes = (
        jax.ShapeDtypeStruct((6, WLON, 2, C), BF),
        jax.ShapeDtypeStruct((6, WLON, 2, C), BF),
        jax.ShapeDtypeStruct((SHARD, 2, 576), F32),
        jax.ShapeDtypeStruct((SHARD, 2, 192), F32),
        jax.ShapeDtypeStruct((SHARD, 2, 768), F32),
        jax.ShapeDtypeStruct((2, 24, 192), F32),
        jax.ShapeDtypeStruct((2, HEADS, 1, 3312), F32),
    )
    outs = pl.pallas_call(
        kernel,
        out_shape=shapes,
        in_specs=[vm, hbm, hbm, hbm, hbm, hbm, vm],
        out_specs=(vm,) * 7,
        scratch_shapes=[
            pltpu.VMEM((6, WLON, 2, C), BF),
            pltpu.VMEM((2, C, 576), BF),
            pltpu.VMEM((2, C, C), BF),
            pltpu.VMEM((2, C, HID), BF),
            pltpu.VMEM((2, C, HID), BF),
            pltpu.SemaphoreType.DMA((5,)),
            pltpu.VMEM((TOK, C), F32),
            pltpu.VMEM((2, TOK, C), BF),
            pltpu.VMEM((2, TOK, C), F32),
            pltpu.VMEM((2, TOK, 1), F32),
            pltpu.VMEM((2, TOK, 576), BF),
            pltpu.VMEM((HEADS, TOK, TOK), BF),
            pltpu.VMEM((HEADS, TOK, 96), BF),
            pltpu.VMEM((2, TOK, C), BF),
            pltpu.VMEM((2, TOK, C), F32),
            pltpu.VMEM((2, TOK, 1), F32),
            pltpu.VMEM((2, TOK, C), BF),
            pltpu.VMEM((2, TOK, HID), BF),
            pltpu.VMEM((2, TOK, HID), BF),
            pltpu.VMEM((2, TOK, HID), BF),
            pltpu.VMEM((2, TOK, 576), BF),
            pltpu.VMEM((2, TOK, C), BF),
            pltpu.VMEM((2, TOK, C), BF),
            pltpu.VMEM((3, 72, 128), F32),
            pltpu.VMEM((2, 1152, 128), F32),
            pltpu.VMEM((1152, 128), F32),
            pltpu.VMEM((2, 1152, 128), F32),
            pltpu.VMEM((1152, 128), F32),
            pltpu.VMEM((HID, HID), BF),
            pltpu.VMEM((8 * RING, C // 2), BF),
            pltpu.VMEM((4, 3, 48, C), BF),
            pltpu.VMEM((4, 3, 48, C), BF),
            pltpu.VMEM((2, 3, 6, C, 128), BF),
            pltpu.VMEM((2, 3, 3, C, 128), BF),
            pltpu.VMEM((2, 3, 2, 2, C // 2, 128), BF),
            pltpu.VMEM((2, 3, 2, 1, C // 2, 128), BF),
            pltpu.VMEM((2, 2 * CHIPS, 2, C // 2, 128), BF),
            pltpu.VMEM((2, 2 * CHIPS, 1, C // 2, 128), BF),
            pltpu.VMEM((2, 2, RING, 16, 128), BF),
            pltpu.VMEM((2, 2, RING, 16, 128), BF),
            pltpu.VMEM((2, 2, 16, 128), BF),
            pltpu.VMEM((2, 2, 6, 16, 128), BF),
            pltpu.VMEM((17, 16, 128), BF),
            pltpu.VMEM((NLON, 16, 128), BF),
            pltpu.VMEM((17, 16, 128), BF),
            pltpu.SemaphoreType.DMA((4, 3)),
            pltpu.SemaphoreType.DMA((4, 3)),
            pltpu.SemaphoreType.DMA((2, 3)),
            pltpu.SemaphoreType.DMA((2, 3)),
            pltpu.SemaphoreType.DMA((2, 2, 3, 2)),
            pltpu.SemaphoreType.DMA((2, 2)),
            pltpu.SemaphoreType.DMA((2, 2)),
            pltpu.SemaphoreType.DMA((2, 2)),
            pltpu.SemaphoreType.DMA((2, 2)),
            pltpu.SemaphoreType.DMA((2, 2)),
            pltpu.SemaphoreType.DMA((17,)),
            pltpu.SemaphoreType.DMA,
            pltpu.SemaphoreType.DMA,
            pltpu.SemaphoreType.DMA((2,)),
        ],
        compiler_params=pltpu.CompilerParams(
            collective_id=0, has_side_effects=True, vmem_limit_bytes=64 * 1024 * 1024
        ),
        name="earth_blocks",
    )(
        inputs.transpose(1, 2, 0, 3),
        cotangent.transpose(1, 2, 0, 3),
        w_qkv,
        w_proj,
        w_up,
        w_down.transpose(0, 2, 1),
        earth_bias.reshape(2, HEADS, 3312),
    )
    result, grad_inputs, g_qkv, g_proj, g_up, g_down, g_bias = outs
    return (
        result.transpose(2, 0, 1, 3),
        grad_inputs.transpose(2, 0, 1, 3),
        g_qkv.transpose(1, 0, 2),
        g_proj.transpose(1, 0, 2),
        g_up.transpose(1, 0, 2),
        g_down,
        g_bias.reshape(2, 1, 1, HEADS, 3312),
    )


def solution(mesh):
    field = P(None, "lat", "lon", None)
    shard = P(None, "lon", None)
    bias = P(None, "lat", None, None, None)
    return jax.shard_map(
        on_device,
        mesh=mesh,
        in_specs=(field, field, P(), P(), P(), P(), bias),
        out_specs=(field, field, shard, shard, shard, shard, bias),
        check_vma=False,
    )
```

time: 90.6 us -> 69.8 us (0.77)
  Pallas kernels: 80.8 us -> 61.7 us
    pallas_call x1, Pallas kernels: 80.8 us -> 61.7 us  [on_device(): pl.pallas_call(kernel, out_shape=shapes, in_specs=[vm, hbm, hbm, hbm, hbm...]
    unnamed x21 -> x20, local copies, waits for them, and re-layouts: 7.92 us -> 6.46 us
where the time goes in v2:
time: 69.8 us; the launch traced here: 69.6 us
  Pallas kernels  61.7 us (88%)
  local copies, waits for them, and re-layouts  7.17 us (10%)
    pallas_call x1, Pallas kernels, on_device(): pl.pallas_call(kernel, out_shape=shapes, in_specs=[vm, hbm, hbm, hbm, hbm...  61.7 us
    unnamed x20, local copies, waits for them, and re-layouts  6.46 us

profile of v2, /device:TPU:1, one launch (start us, length us, event | category | flops | bytes accessed | tf_op | source)
XLA Modules:
  0.0 69.6 jit_solution(7451285967626075054)
XLA Ops:
  0.6 1.0 %copy.19 = f32[2,1,1,6,3312]{4,0,3,2,1:T(2,128)S(1)} copy(f32[2,1,1,6,3312]{4,2,3,1,0:T(1,128)} %param.13) | data formatting | bytes 317952 | tf_op args[6]
  1.6 0.7 %copy.16.eb_ref = f32[2,6,3312]{2,1,0:T(8,128)} copy(f32[2,6,3312]{2,0,1:T(2,128)S(1)} %bitcast.14) | data formatting | bytes 317952 | tf_op jit(solution)/shard_map/reshape | solution.py:873
  2.3 61.7 %earth_blocks.1 = (bf16[6,12,2,192]{3,2,1,0:T(2,128)(2,1)}, bf16[6,12,2,192]{3,2,1,0:T(2,128)(2,1)}, f32[6,2,576]{2,1,0:T(2,128)}, f32[6,2,192]{2,1,0:T(2,128)},...) custom-call(bf16[6,12,2,192]{3,2,1,0:T(2,128)(2,1)} %bitcast.17, ...), custom_call_target="tpu_custom_call" | custom-call | tf_op jit(solution)/shard_map/earth_blocks/pallas_call | solution.py:796
  64.1 0.0 copy-start.1
  64.1 1.6 %copy.27 = bf16[2,6,12,192]{3,0,2,1:T(2,128)(2,1)} copy(bf16[2,6,12,192]{3,0,2,1:T(2,128)(2,1)} %bitcast.20) | data formatting | bytes 110592
  65.7 0.0 copy-done.1
  65.7 0.0 copy-start.4
  65.7 0.0 copy-start.5
  65.7 0.0 copy-start.3
  65.7 0.0 copy-start.2
  65.7 0.6 copy.28
  66.3 0.1 copy-done.4
  66.4 0.0 copy-start
  66.4 0.6 copy.29
  67.0 0.0 copy-done.5
  67.0 0.6 copy.30
  67.6 0.0 copy-done.3
  67.6 0.6 copy.31
  68.3 0.0 copy-done.2
  68.3 0.6 copy.32
  68.9 0.0 copy-done
  68.9 0.7 copy.33
Async XLA Ops:
  64.1 1.6 %copy-start.1 = (bf16[6,12,2,192]{3,2,1,0:T(2,128)(2,1)S(1)}, bf16[6,12,2,192]{3,2,1,0:T(2,128)(2,1)}, u32[]{:S(2)}) copy-start(bf16[6,12,2,192]{3,2,1,0:T(2,128)(2,1)} %get-tuple-element.15) | copy-start | bytes 165892
  65.7 0.8 %copy-start.4 = (f32[6,2,576]{2,1,0:T(2,128)S(1)}, f32[6,2,576]{2,1,0:T(2,128)}, u32[]{:S(2)}) copy-start(f32[6,2,576]{2,1,0:T(2,128)} %get-tuple-element.16) | copy-start | bytes 82948
  65.7 1.4 %copy-start.5 = (f32[6,2,192]{2,1,0:T(2,128)S(1)}, f32[6,2,192]{2,1,0:T(2,128)}, u32[]{:S(2)}) copy-start(f32[6,2,192]{2,1,0:T(2,128)} %get-tuple-element.17) | copy-start | bytes 27652
  65.7 2.0 %copy-start.3 = (f32[6,2,768]{2,1,0:T(2,128)S(1)}, f32[6,2,768]{2,1,0:T(2,128)}, u32[]{:S(2)}) copy-start(f32[6,2,768]{2,1,0:T(2,128)} %get-tuple-element.18) | copy-start | bytes 110596
  65.7 2.6 %copy-start.2 = (f32[2,24,192]{2,1,0:T(8,128)S(1)}, f32[2,24,192]{2,1,0:T(8,128)}, u32[]{:S(2)}) copy-start(f32[2,24,192]{2,1,0:T(8,128)} %get-tuple-element.47) | copy-start | bytes 110596
  66.4 2.5 %copy-start = (f32[2,6,1,3312]{3,2,1,0:T(1,128)S(1)}, f32[2,6,1,3312]{3,2,1,0:T(1,128)}, u32[]{:S(2)}) copy-start(f32[2,6,1,3312]{3,2,1,0:T(1,128)} %get-tuple-element.20) | copy-start | bytes 476932

commit v3 on v2

--- a/solution.py
+++ b/solution.py
@@ -297,22 +297,29 @@
         sc1_ref[b] = sc1
         inv1_ref[b] = inv1
         qkv_ref[b] = nn(n1, wqkv_ref[b]).astype(BF)
+        q = qkv_ref[b, :, 0:C]
+        k = qkv_ref[b, :, C:2 * C]
+        v = qkv_ref[b, :, 2 * C:3 * C]
+        cases = [(seg, slice(start, start + size), h) for seg, (start, size) in enumerate(segments[b]) for h in range(HEADS)]
+        qh = [q * hm[h] for h in range(HEADS)]
+        vh = [v * hm[h] for h in range(HEADS)]
+        scores = [nt(qh[h][rows], k[rows]) for _, rows, h in cases]
+        probs = []
+        for (seg, rows, h), raw in zip(cases, scores):
+            full = raw * SCALE + head_bias(b, h, seg)
+            e = jnp.exp(full - jnp.max(full, axis=-1, keepdims=True))
+            p = (e * (1.0 / jnp.sum(e, axis=-1, keepdims=True))).astype(BF)
+            if b == 0:
+                p1_ref[h] = p
+            else:
+                p2_ref[h, rows, :] = p
+            probs.append(p)
+        mixed = [None] * len(segments[b])
+        for (seg, rows, h), p in zip(cases, probs):
+            part = nn(p, vh[h][rows])
+            mixed[seg] = part if h == 0 else mixed[seg] + part
         for seg, (start, size) in enumerate(segments[b]):
-            q = qkv_ref[b, start:start + size, 0:C]
-            k = qkv_ref[b, start:start + size, C:2 * C]
-            v = qkv_ref[b, start:start + size, 2 * C:3 * C]
-            mixed = jnp.zeros((size, C), F32)
-            for h in range(HEADS):
-                scores = nt(q * hm[h], k) * SCALE + head_bias(b, h, seg)
-                top = jnp.max(scores, axis=-1, keepdims=True)
-                e = jnp.exp(scores - top)
-                probs = (e * (1.0 / jnp.sum(e, axis=-1, keepdims=True))).astype(BF)
-                if b == 0:
-                    p1_ref[h] = probs
-                else:
-                    p2_ref[h, start:start + size, :] = probs
-                mixed = mixed + nn(probs, v * hm[h])
-            mix_ref[b, start:start + size, :] = mixed.astype(BF)
+            mix_ref[b, start:start + size, :] = mixed[seg].astype(BF)
         hidden = (u + nn(mix_ref[b], wproj_ref[b])).astype(BF).astype(F32)
         sc2, inv2 = ln(hidden)
         n2 = sc2.astype(BF)
@@ -341,38 +348,48 @@
         ghb_ref[b] = ghid.astype(BF)
         return ghid
 
-    def attention_grads(b):
-        gmix_all = nt(ghb_ref[b], wproj_ref[b]).astype(BF)
+    def attention_start(b):
+        gmix = nt(ghb_ref[b], wproj_ref[b]).astype(BF)
+        q = qkv_ref[b, :, 0:C]
+        v = qkv_ref[b, :, 2 * C:3 * C]
+        cases = [(seg, slice(start, start + size), h) for seg, (start, size) in enumerate(segments[b]) for h in range(HEADS)]
+        gh = [gmix * hm[h] for h in range(HEADS)]
+        gps = [nt(gh[h][rows], v[rows]) for _, rows, h in cases]
+        spans = [slice(start, start + size) for start, size in segments[b]]
+        qt = [nt(eye, q[rows]).astype(BF) for rows in spans]
+        gmt = [nt(eye, gmix[rows]).astype(BF) for rows in spans]
+        return cases, gps, qt, gmt
+
+    def attention_grads(b, started):
+        cases, gps, qt, gmt = started
+        k = qkv_ref[b, :, C:2 * C]
+        kh = [k * hm[h] for h in range(HEADS)]
+        gvt = []
+        dsbs = []
+        for (seg, rows, h), gp in zip(cases, gps):
+            pb = p1_ref[h] if b == 0 else p2_ref[h, rows, :]
+            gvt.append(nn(gmt[seg][32 * h:32 * h + 32], pb))
+            pf = pb.astype(F32)
+            ds = pf * (gp - jnp.sum(gp * pf, axis=-1, keepdims=True))
+            if b == 0:
+                ds1_ref[0, TOK * h:TOK * h + TOK, :] = ds[:, 0:128]
+                ds1_ref[1, TOK * h:TOK * h + TOK, 0:64] = ds[:, 128:192]
+            else:
+                at = 96 * (HEADS * seg + h)
+                ds2_ref[at:at + 96, 0:96] = ds
+            dsbs.append(ds.astype(BF))
+        gkt = [nn(qt[seg][32 * h:32 * h + 32], dsb) for (seg, _, h), dsb in zip(cases, dsbs)]
+        gq = [None] * len(segments[b])
+        for (seg, rows, h), dsb in zip(cases, dsbs):
+            part = nn(dsb, kh[h][rows])
+            gq[seg] = part if h == 0 else gq[seg] + part
         for seg, (start, size) in enumerate(segments[b]):
             rows = slice(start, start + size)
-            q = qkv_ref[b, rows, 0:C]
-            k = qkv_ref[b, rows, C:2 * C]
-            v = qkv_ref[b, rows, 2 * C:3 * C]
-            gmix = gmix_all[rows]
-            qt = nt(eye, q).astype(BF)
-            gmt = nt(eye, gmix).astype(BF)
-            gq = jnp.zeros((size, C), F32)
-            gkt = []
-            gvt = []
-            for h in range(HEADS):
-                pb = p1_ref[h] if b == 0 else p2_ref[h, rows, :]
-                pf = pb.astype(F32)
-                gp = nt(gmix * hm[h], v)
-                ds = pf * (gp - jnp.sum(gp * pf, axis=-1, keepdims=True))
-                if b == 0:
-                    ds1_ref[0, TOK * h:TOK * h + TOK, :] = ds[:, 0:128]
-                    ds1_ref[1, TOK * h:TOK * h + TOK, 0:64] = ds[:, 128:192]
-                else:
-                    at = 96 * (HEADS * seg + h)
-                    ds2_ref[at:at + 96, 0:96] = ds
-                dsb = ds.astype(BF)
-                gq = gq + nn(dsb, k * hm[h])
-                gkt.append(nn(qt[32 * h:32 * h + 32], dsb))
-                gvt.append(nn(gmt[32 * h:32 * h + 32], pb))
+            heads = slice(HEADS * seg, HEADS * seg + HEADS)
             small = eye if size == C else eye[0:size, 0:size]
-            gk = nt(small, (jnp.concatenate(gkt, axis=0) * SCALE).astype(BF)).astype(BF)
-            gv = nt(small, jnp.concatenate(gvt, axis=0).astype(BF)).astype(BF)
-            gqkv_ref[b, rows, 0:C] = (gq * SCALE).astype(BF)
+            gk = nt(small, (jnp.concatenate(gkt[heads], axis=0) * SCALE).astype(BF)).astype(BF)
+            gv = nt(small, jnp.concatenate(gvt[heads], axis=0).astype(BF)).astype(BF)
+            gqkv_ref[b, rows, 0:C] = (gq[seg] * SCALE).astype(BF)
             gqkv_ref[b, rows, C:2 * C] = gk
             gqkv_ref[b, rows, 2 * C:3 * C] = gv
 
@@ -410,6 +427,11 @@
     z = lax.rem(lon, RING)
     half = C // 2
     a_refs = (a_du_ref, a_qp_ref)
+
+    def far_first(i):
+        step = (i + 1) // 2
+        return lax.rem(z + RING // 2 + step * (1 - 2 * lax.rem(i, 2)), RING)
+
     r1_refs = (r1_du_ref, r1_qp_ref)
 
     def place(b):
@@ -499,8 +521,8 @@
                 s2_ref[b, kind, j] = tile.astype(BF)
             r2_ref[b, kind, z] = s2_ref[b, kind, z]
 
-            def send(k, carry):
-                to = lax.rem(z + k, RING)
+            def send(i, carry):
+                to = far_first(i)
                 pltpu.make_async_remote_copy(
                     src_ref=s2_ref.at[b, kind, to],
                     dst_ref=r2_ref.at[b, kind, z],
@@ -511,7 +533,7 @@
                 ).start()
                 return carry
 
-            lax.fori_loop(1, RING, send, 0)
+            lax.fori_loop(0, RING - 1, send, 0)
 
     def stage2_reduce(b, kind):
         mine, i = owned(b, kind)
@@ -657,18 +679,24 @@
                 acc = acc + br_ref[j].astype(F32)
             ball_ref[at] = acc.astype(BF)
 
-            def send(k, carry):
+            def send_to(to):
                 pltpu.make_async_remote_copy(
                     src_ref=ball_ref.at[at],
                     dst_ref=ball_ref.at[at],
                     send_sem=bg_send,
                     recv_sem=bg_recv.at[b],
-                    device_id={"lon": at_lon(k)},
+                    device_id={"lon": to},
                     device_id_type=MESH,
                 ).start()
+
+            def send(i, carry):
+                to = far_first(i)
+                send_to(RING * (1 - ring) + to)
+                send_to(RING * ring + to)
                 return carry
 
-            lax.fori_loop(1, NLON, send, 0)
+            lax.fori_loop(0, RING - 1, send, 0)
+            send_to(RING * (1 - ring) + z)
 
     def bias_finish(b):
         mine, _ = bias_mine(b)
@@ -734,7 +762,7 @@
     exchange_start(2, out2)
     g2 = exchange_finish(0, ct)
     ghid2 = backward_mlp(1, g2)
-    attention_grads(1)
+    attention_grads(1, attention_start(1))
     gsec = input_grad(1, ghid2)
     exchange_start(3, gsec)
     grads_mlp(1)
@@ -752,15 +780,16 @@
     grads_mlp(0)
     stage0_send(0, 0)
     stage0_send(0, 1)
-    attention_grads(0)
+    started = attention_start(0)
+    stage1_send(0, 0)
+    attention_grads(0, started)
+    grads_attention(0)
+    stage0_send(0, 2)
     fold_bias(0)
     bias_send(0)
-    grads_attention(0)
-    stage0_send(0, 2)
-    stage1_send(0, 0)
+    stage1_send(0, 1)
     stage1_reduce(1, 0)
     stage1_reduce(1, 1)
-    stage1_send(0, 1)
     bias_reduce(1)
     store_window(gin_ref, input_grad(0, ghid1))
     stage1_reduce(0, 0)

time: 69.8 us -> 66.8 us (0.957)
  Pallas kernels: 61.7 us -> 58.7 us
    pallas_call x1, Pallas kernels: 61.7 us -> 58.7 us  [on_device(): pl.pallas_call(kernel, out_shape=shapes, in_specs=[vm, hbm, hbm, hbm, hbm...]
where the time goes in v3:
time: 66.8 us; the launch traced here: 66.5 us
  Pallas kernels  58.7 us (88%)
  local copies, waits for them, and re-layouts  7.17 us (11%)
  between operations  0.67 us (1%)
    pallas_call x1, Pallas kernels, on_device(): pl.pallas_call(kernel, out_shape=shapes, in_specs=[vm, hbm, hbm, hbm, hbm...  58.7 us
    unnamed x20, local copies, waits for them, and re-layouts  6.46 us

profile of v3, /device:TPU:1, one launch (start us, length us, event | category | flops | bytes accessed | tf_op | source)
XLA Modules:
  0.0 66.5 jit_solution(3218864379038770979)
XLA Ops:
  0.6 1.0 %copy.19 = f32[2,1,1,6,3312]{4,0,3,2,1:T(2,128)S(1)} copy(f32[2,1,1,6,3312]{4,2,3,1,0:T(1,128)} %param.13) | data formatting | bytes 317952 | tf_op args[6]
  1.6 0.7 %copy.16.eb_ref = f32[2,6,3312]{2,1,0:T(8,128)} copy(f32[2,6,3312]{2,0,1:T(2,128)S(1)} %bitcast.14) | data formatting | bytes 317952 | tf_op jit(solution)/shard_map/reshape | solution.py:902
  2.3 58.7 %earth_blocks.1 = (bf16[6,12,2,192]{3,2,1,0:T(2,128)(2,1)}, bf16[6,12,2,192]{3,2,1,0:T(2,128)(2,1)}, f32[6,2,576]{2,1,0:T(2,128)}, f32[6,2,192]{2,1,0:T(2,128)},...) custom-call(bf16[6,12,2,192]{3,2,1,0:T(2,128)(2,1)} %bitcast.17, ...), custom_call_target="tpu_custom_call" | custom-call | tf_op jit(solution)/shard_map/earth_blocks/pallas_call | solution.py:825
  61.0 0.0 copy-start.1
  61.0 1.6 %copy.27 = bf16[2,6,12,192]{3,0,2,1:T(2,128)(2,1)} copy(bf16[2,6,12,192]{3,0,2,1:T(2,128)(2,1)} %bitcast.20) | data formatting | bytes 110592
  62.6 0.0 copy-done.1
  62.6 0.0 copy-start.4
  62.6 0.0 copy-start.5
  62.6 0.0 copy-start.3
  62.6 0.0 copy-start.2
  62.6 0.6 copy.28
  63.3 0.1 copy-done.4
  63.4 0.0 copy-start
  63.4 0.6 copy.29
  64.0 0.0 copy-done.5
  64.0 0.6 copy.30
  64.6 0.0 copy-done.3
  64.6 0.6 copy.31
  65.2 0.0 copy-done.2
  65.2 0.6 copy.32
  65.8 0.0 copy-done
  65.8 0.7 copy.33
Async XLA Ops:
  61.0 1.6 %copy-start.1 = (bf16[6,12,2,192]{3,2,1,0:T(2,128)(2,1)S(1)}, bf16[6,12,2,192]{3,2,1,0:T(2,128)(2,1)}, u32[]{:S(2)}) copy-start(bf16[6,12,2,192]{3,2,1,0:T(2,128)(2,1)} %get-tuple-element.15) | copy-start | bytes 165892
  62.6 0.8 %copy-start.4 = (f32[6,2,576]{2,1,0:T(2,128)S(1)}, f32[6,2,576]{2,1,0:T(2,128)}, u32[]{:S(2)}) copy-start(f32[6,2,576]{2,1,0:T(2,128)} %get-tuple-element.16) | copy-start | bytes 82948
  62.6 1.4 %copy-start.5 = (f32[6,2,192]{2,1,0:T(2,128)S(1)}, f32[6,2,192]{2,1,0:T(2,128)}, u32[]{:S(2)}) copy-start(f32[6,2,192]{2,1,0:T(2,128)} %get-tuple-element.17) | copy-start | bytes 27652
  62.6 2.0 %copy-start.3 = (f32[6,2,768]{2,1,0:T(2,128)S(1)}, f32[6,2,768]{2,1,0:T(2,128)}, u32[]{:S(2)}) copy-start(f32[6,2,768]{2,1,0:T(2,128)} %get-tuple-element.18) | copy-start | bytes 110596
  62.6 2.6 %copy-start.2 = (f32[2,24,192]{2,1,0:T(8,128)S(1)}, f32[2,24,192]{2,1,0:T(8,128)}, u32[]{:S(2)}) copy-start(f32[2,24,192]{2,1,0:T(8,128)} %get-tuple-element.47) | copy-start | bytes 110596
  63.4 2.5 %copy-start = (f32[2,6,1,3312]{3,2,1,0:T(1,128)S(1)}, f32[2,6,1,3312]{3,2,1,0:T(1,128)}, u32[]{:S(2)}) copy-start(f32[2,6,1,3312]{3,2,1,0:T(1,128)} %get-tuple-element.20) | copy-start | bytes 476932

commit v4 on v3

--- a/solution.py
+++ b/solution.py
@@ -194,7 +194,7 @@
             parts = (strip(val, 3, 0), strip(val, 0, 1), strip(val, 0, 0))
         else:
             parts = (strip(val, 0, 1), strip(val, 3, 0), strip(val, 3, 1))
-        for i, copy in enumerate(exchange_copies(idx)):
+        for i, copy in reversed(list(enumerate(exchange_copies(idx)))):
             xs_ref[idx, i] = parts[i]
             copy.start()
 
@@ -236,7 +236,7 @@
             for lt in range(3):
                 width = min(128, TAB - 128 * lt)
                 lane = TAB * a + 128 * lt
-                piece = eb_ref[b, :, lane:lane + width]
+                piece = eb_ref[:, b, lane:lane + width]
                 if width < 128:
                     piece = jnp.concatenate([piece, jnp.zeros((HEADS, 128 - width), F32)], axis=1)
                 t_ref[lt, rows, :] = piece
@@ -434,6 +434,10 @@
 
     r1_refs = (r1_du_ref, r1_qp_ref)
 
+    def far_first_lat(i):
+        step = (i + 1) // 2
+        return lax.rem(lat + NLAT // 2 + step * (1 - 2 * lax.rem(i, 2)), NLAT)
+
     def place(b):
         return chip if b else lax.rem(chip + 4, 8)
 
@@ -549,18 +553,18 @@
             s3_ref[b, kind] = total
             r3_ref[b, kind, which] = total
 
-            def send(k, carry):
+            def send(i, carry):
                 pltpu.make_async_remote_copy(
                     src_ref=s3_ref.at[b, kind],
                     dst_ref=r3_ref.at[b, kind, which],
                     send_sem=s3_send.at[b, kind],
                     recv_sem=s3_recv.at[b, kind],
-                    device_id={"lat": at_lat(k)},
+                    device_id={"lat": far_first_lat(i)},
                     device_id_type=MESH,
                 ).start()
                 return carry
 
-            lax.fori_loop(1, NLAT, send, 0)
+            lax.fori_loop(0, NLAT - 1, send, 0)
 
     def put_rows(ref, b, val):
         for i in range(SHARD):
@@ -899,7 +903,7 @@
         w_proj,
         w_up,
         w_down.transpose(0, 2, 1),
-        earth_bias.reshape(2, HEADS, 3312),
+        earth_bias.reshape(2, HEADS, 3312).transpose(1, 0, 2),
     )
     result, grad_inputs, g_qkv, g_proj, g_up, g_down, g_bias = outs
     return (

time: 66.8 us -> 66.1 us (0.990)
  Pallas kernels: 58.7 us -> 58 us
    reshape x1 -> x0, local copies, waits for them, and re-layouts: 0.7 us -> none  [on_device(): earth_bias.reshape(2, HEADS, 3312)]
where the time goes in v4:
time: 66.1 us; the launch traced here: 65.8 us
  Pallas kernels  58 us (88%)
  local copies, waits for them, and re-layouts  7.13 us (11%)
  between operations  0.67 us (1%)
    pallas_call x1, Pallas kernels, on_device(): pl.pallas_call(kernel, out_shape=shapes, in_specs=[vm, hbm, hbm, hbm, hbm...  58 us
    unnamed x20, local copies, waits for them, and re-layouts  7.13 us

profile of v4, /device:TPU:1, one launch (start us, length us, event | category | flops | bytes accessed | tf_op | source)
XLA Modules:
  0.0 65.8 jit_solution(1519344638916093148)
XLA Ops:
  0.6 1.7 %copy.17 = f32[2,1,1,6,3312]{4,0,3,2,1:T(2,128)} copy(f32[2,1,1,6,3312]{4,2,3,1,0:T(1,128)} %param.13) | data formatting | bytes 317952 | tf_op args[6]
  2.3 58.0 %earth_blocks.1 = (bf16[6,12,2,192]{3,2,1,0:T(2,128)(2,1)}, bf16[6,12,2,192]{3,2,1,0:T(2,128)(2,1)}, f32[6,2,576]{2,1,0:T(2,128)}, f32[6,2,192]{2,1,0:T(2,128)},...) custom-call(bf16[6,12,2,192]{3,2,1,0:T(2,128)(2,1)} %bitcast.19, ...), custom_call_target="tpu_custom_call" | custom-call | tf_op jit(solution)/shard_map/earth_blocks/pallas_call | solution.py:829
  60.3 0.0 copy-start.1
  60.3 1.6 %copy.25 = bf16[2,6,12,192]{3,0,2,1:T(2,128)(2,1)} copy(bf16[2,6,12,192]{3,0,2,1:T(2,128)(2,1)} %bitcast.22) | data formatting | bytes 110592
  61.9 0.0 copy-done.1
  61.9 0.0 copy-start.4
  61.9 0.0 copy-start.5
  61.9 0.0 copy-start.3
  61.9 0.0 copy-start.2
  62.0 0.6 copy.26
  62.6 0.1 copy-done.4
  62.7 0.0 copy-start
  62.7 0.6 copy.27
  63.3 0.0 copy-done.5
  63.3 0.6 copy.28
  63.9 0.0 copy-done.3
  63.9 0.6 copy.29
  64.5 0.0 copy-done.2
  64.5 0.6 copy.30
  65.1 0.0 copy-done
  65.1 0.7 %copy.31 = f32[2,1,1,6,3312]{4,2,3,1,0:T(1,128)} copy(f32[2,1,1,6,3312]{4,2,3,1,0:T(1,128)S(1)} %bitcast.18) | data formatting | bytes 317952
Async XLA Ops:
  60.3 1.6 %copy-start.1 = (bf16[6,12,2,192]{3,2,1,0:T(2,128)(2,1)S(1)}, bf16[6,12,2,192]{3,2,1,0:T(2,128)(2,1)}, u32[]{:S(2)}) copy-start(bf16[6,12,2,192]{3,2,1,0:T(2,128)(2,1)} %get-tuple-element.15) | copy-start | bytes 165892
  61.9 0.8 %copy-start.4 = (f32[6,2,576]{2,1,0:T(2,128)S(1)}, f32[6,2,576]{2,1,0:T(2,128)}, u32[]{:S(2)}) copy-start(f32[6,2,576]{2,1,0:T(2,128)} %get-tuple-element.16) | copy-start | bytes 82948
  61.9 1.4 %copy-start.5 = (f32[6,2,192]{2,1,0:T(2,128)S(1)}, f32[6,2,192]{2,1,0:T(2,128)}, u32[]{:S(2)}) copy-start(f32[6,2,192]{2,1,0:T(2,128)} %get-tuple-element.17) | copy-start | bytes 27652
  61.9 2.0 %copy-start.3 = (f32[6,2,768]{2,1,0:T(2,128)S(1)}, f32[6,2,768]{2,1,0:T(2,128)}, u32[]{:S(2)}) copy-start(f32[6,2,768]{2,1,0:T(2,128)} %get-tuple-element.18) | copy-start | bytes 110596
  61.9 2.6 %copy-start.2 = (f32[2,24,192]{2,1,0:T(8,128)S(1)}, f32[2,24,192]{2,1,0:T(8,128)}, u32[]{:S(2)}) copy-start(f32[2,24,192]{2,1,0:T(8,128)} %get-tuple-element.40) | copy-start | bytes 110596
  62.7 2.5 %copy-start = (f32[2,6,1,3312]{3,2,1,0:T(1,128)S(1)}, f32[2,6,1,3312]{3,2,1,0:T(1,128)}, u32[]{:S(2)}) copy-start(f32[2,6,1,3312]{3,2,1,0:T(1,128)} %get-tuple-element.20) | copy-start | bytes 476932
